TPU v7x, 32 devices: a whole 2x2x4 slice. The times are simulated.
32 devices in a mesh: dp: 2 (over core), fsdp: 4 (over y, x), ctx: 4 (over z).
Axes of the slice: x: 2, y: 2, z: 4, core: 2. Of those that a mesh axis runs over, the one named last changes fastest.
Arguments:
- tokens: bfloat16 [8, 1024, 960], P(('dp', 'fsdp'), 'ctx'), may hold values from -6 to 6
- positions: int32 [8, 1024], P(('dp', 'fsdp'), 'ctx'), may hold values from 0 to 2046, as said below
- gain_attn: float32 [960], replicated, may hold values from 0.25 to 1.75
- gain_mlp: float32 [960], replicated, may hold values from 0.25 to 1.75
- w_qkv: bfloat16 [960, 1600], P('fsdp'), may hold values from -0.1875 to 0.1875
- w_out: bfloat16 [960, 960], P('fsdp'), may hold values from -0.75 to 0.75
- w_gu: bfloat16 [960, 5120], P('fsdp'), may hold values from -0.1875 to 0.1875
- w_down: bfloat16 [2560, 960], P('fsdp'), may hold values from -0.125 to 0.125
- cotangent: bfloat16 [8, 1024, 960], P(('dp', 'fsdp'), 'ctx'), may hold values from -6 to 6
Outputs:
- out_tokens: float32 [8, 1024, 960], P(('dp', 'fsdp'), 'ctx')
- grad_tokens: float32 [8, 1024, 960], P(('dp', 'fsdp'), 'ctx')
- grad_gain_attn: float32 [960], P(('fsdp', 'ctx'))
- grad_gain_mlp: float32 [960], P(('fsdp', 'ctx'))
- grad_qkv: float32 [960, 1600], P(('fsdp', 'ctx'), 'dp')
- grad_out: float32 [960, 960], P(('fsdp', 'ctx'), 'dp')
- grad_gu: float32 [960, 5120], P(('fsdp', 'ctx'), 'dp')
- grad_down: float32 [2560, 960], P(('fsdp', 'ctx'), 'dp')
Inputs may be any that keep to these rules, and one draw needn't show every extreme that they name: `positions`: strictly increasing along each sequence; each sequence starts at 0 and ends at 2046.
All inputs are finite; a program needn't handle non-finite values.
Results may differ from a plain program's by a relative error of at most 0.02.
Values may be sent and summed in bfloat16 or wider, within the bound.
A program may use at most 128 MiB of HBM per device.

v0:
```python
import jax
import jax.numpy as jnp
from jax import lax
from jax.sharding import PartitionSpec as P

D = 960
HEADS = 15
KV_HEADS = 5
HD = 64
FF = 2560


EPSILON = 1e-05


def rotate(values, places, direction):
    half_dim = values.shape[-1] // 2
    frequency = 10000.0 ** (-jnp.arange(half_dim, dtype=jnp.float32) / half_dim)
    angles = places.astype(jnp.float32)[:, None] * frequency[None, :]
    cosine = jnp.cos(angles)[:, None, :]
    sine_part = direction * jnp.sin(angles)[:, None, :]
    front_half = values[..., :half_dim]
    back_half = values[..., half_dim:]
    return jnp.concatenate(
        [front_half * cosine - back_half * sine_part, back_half * cosine + front_half * sine_part],
        axis=-1,
    )


def normalize(values, gain):
    return values * lax.rsqrt(jnp.mean(values * values, axis=-1, keepdims=True) + EPSILON) * gain


def split_heads(every_kv):
    length = every_kv.shape[0]
    kv_width = KV_HEADS * HD
    key_heads = every_kv[:, :kv_width].reshape(length, KV_HEADS, HD).transpose(1, 0, 2)
    value_heads = every_kv[:, kv_width:].reshape(length, KV_HEADS, HD).transpose(1, 0, 2)
    return (key_heads, value_heads)


def masked_scores(queries, key_block, row_start):
    scores = HD ** (-0.5) * jnp.einsum(
        "qgd,sd->gqs", queries, key_block, preferred_element_type=jnp.float32
    )
    allowed = (
        jnp.arange(key_block.shape[0])[None, None, :]
        <= (row_start + jnp.arange(queries.shape[0]))[None, :, None]
    )
    return jnp.where(allowed, scores, -1e30)


def head_forward(queries, key_block, values, row_start):
    scores = masked_scores(queries, key_block, row_start)
    row_max = jnp.max(scores, axis=-1, keepdims=True)
    exponent = jnp.exp(scores - row_max)
    row_total = jnp.sum(exponent, axis=-1, keepdims=True)
    probability = (exponent / row_total).astype(jnp.bfloat16)
    attended = jnp.einsum("gqs,sd->qgd", probability, values, preferred_element_type=jnp.float32)
    return (attended, row_max, row_total)


def head_backward(queries, key_block, values, grad_attended, row_max, row_total, row_start):
    scores = masked_scores(queries, key_block, row_start)
    probability = jnp.exp(scores - row_max) / row_total
    grad_probs = jnp.einsum(
        "qgd,sd->gqs", grad_attended, values, preferred_element_type=jnp.float32
    )
    inner_sum = jnp.sum(grad_probs * probability, axis=-1, keepdims=True)
    grad_scores = (probability * (grad_probs - inner_sum)).astype(jnp.bfloat16)
    grad_queries = HD ** (-0.5) * jnp.einsum(
        "gqs,sd->qgd", grad_scores, key_block, preferred_element_type=jnp.float32
    )
    grad_keys = HD ** (-0.5) * jnp.einsum(
        "gqs,qgd->sd", grad_scores, queries, preferred_element_type=jnp.float32
    )
    grad_values = jnp.einsum(
        "gqs,qgd->sd",
        probability.astype(jnp.bfloat16),
        grad_attended,
        preferred_element_type=jnp.float32,
    )
    return (grad_queries, grad_keys, grad_values)


def shards(tokens, positions, gain_attn, gain_mlp, w_qkv, w_out, w_gu, w_down, cotangent):
    row_count = tokens.shape[1]
    kv_width = KV_HEADS * HD
    group_size = HEADS // KV_HEADS
    row_start = lax.axis_index("ctx") * row_count
    inputs = tokens[0].astype(jnp.float32)
    places = positions[0]
    full_qkv, full_out, full_gu, full_down = (
        lax.all_gather(w_qkv, "fsdp", axis=0, tiled=True),
        lax.all_gather(w_out, "fsdp", axis=0, tiled=True),
        lax.all_gather(w_gu, "fsdp", axis=0, tiled=True),
        lax.all_gather(w_down, "fsdp", axis=0, tiled=True),
    )
    normed = normalize(inputs, gain_attn).astype(jnp.bfloat16)
    project = jnp.dot(normed, full_qkv, preferred_element_type=jnp.float32)
    queries = rotate(project[:, :D].reshape(row_count, HEADS, HD), places, 1.0).astype(jnp.bfloat16)
    key_block = rotate(
        project[:, D : D + kv_width].reshape(row_count, KV_HEADS, HD), places, 1.0
    ).astype(jnp.bfloat16)
    values = project[:, D + kv_width :].astype(jnp.bfloat16)
    local_kv = jnp.concatenate([key_block.reshape(row_count, kv_width), values], axis=1)
    every_kv = lax.all_gather(local_kv, "ctx", axis=0, tiled=True)
    key_heads, value_heads = split_heads(every_kv)
    query_heads = queries.reshape(row_count, KV_HEADS, group_size, HD).transpose(1, 0, 2, 3)
    attended_heads, row_maxes, row_totals = lax.map(
        lambda packed: head_forward(packed[0], packed[1], packed[2], row_start),
        (query_heads, key_heads, value_heads),
    )
    attended = attended_heads.transpose(1, 0, 2, 3).reshape(row_count, D).astype(jnp.bfloat16)
    hidden_state = inputs + jnp.dot(attended, full_out, preferred_element_type=jnp.float32)
    normed_two = normalize(hidden_state, gain_mlp).astype(jnp.bfloat16)
    gate_up = jnp.dot(normed_two, full_gu, preferred_element_type=jnp.float32)
    gate_part = gate_up[:, :FF]
    up_part = gate_up[:, FF:]
    activated = (jax.nn.silu(gate_part) * up_part).astype(jnp.bfloat16)
    outputs = hidden_state + jnp.dot(activated, full_down, preferred_element_type=jnp.float32)
    full_qkv, full_out, full_gu, full_down = (
        lax.all_gather(w_qkv, "fsdp", axis=0, tiled=True),
        lax.all_gather(w_out, "fsdp", axis=0, tiled=True),
        lax.all_gather(w_gu, "fsdp", axis=0, tiled=True),
        lax.all_gather(w_down, "fsdp", axis=0, tiled=True),
    )
    every_kv = lax.all_gather(local_kv, "ctx", axis=0, tiled=True)
    key_heads, value_heads = split_heads(every_kv)
    grad_rows = cotangent[0].astype(jnp.float32)
    grad_branch = grad_rows.astype(jnp.bfloat16)
    grad_activated = jnp.dot(grad_branch, full_down.T, preferred_element_type=jnp.float32)
    grad_down = jnp.dot(activated.T, grad_branch, preferred_element_type=jnp.float32)
    unused_value, swish_back = jax.vjp(
        lambda gate_in, up_in: jax.nn.silu(gate_in) * up_in, gate_part, up_part
    )
    grad_gate, grad_up = swish_back(grad_activated)
    grad_gate_up = jnp.concatenate([grad_gate, grad_up], axis=1).astype(jnp.bfloat16)
    grad_normed_two = jnp.dot(grad_gate_up, full_gu.T, preferred_element_type=jnp.float32)
    grad_gu = jnp.dot(normed_two.T, grad_gate_up, preferred_element_type=jnp.float32)
    unused_norm, norm_back_two = jax.vjp(normalize, hidden_state, gain_mlp)
    grad_hidden_part, grad_gain_mlp = norm_back_two(grad_normed_two)
    grad_hidden = grad_rows + grad_hidden_part
    grad_attn = grad_hidden.astype(jnp.bfloat16)
    grad_attended = jnp.dot(grad_attn, full_out.T, preferred_element_type=jnp.float32).astype(
        jnp.bfloat16
    )
    grad_out_weight = jnp.dot(attended.T, grad_attn, preferred_element_type=jnp.float32)
    grad_attended_heads = grad_attended.reshape(row_count, KV_HEADS, group_size, HD).transpose(
        1, 0, 2, 3
    )
    grad_query_heads, grad_key_heads, grad_value_heads = lax.map(
        lambda packed: head_backward(
            packed[0], packed[1], packed[2], packed[3], packed[4], packed[5], row_start
        ),
        (query_heads, key_heads, value_heads, grad_attended_heads, row_maxes, row_totals),
    )
    length = every_kv.shape[0]
    kv_grads_all = jnp.concatenate(
        [
            grad_key_heads.transpose(1, 0, 2).reshape(length, kv_width),
            grad_value_heads.transpose(1, 0, 2).reshape(length, kv_width),
        ],
        axis=1,
    )
    own_kv_grads = lax.psum_scatter(
        kv_grads_all.astype(jnp.bfloat16), "ctx", scatter_dimension=0, tiled=True
    ).astype(jnp.float32)
    grad_queries = grad_query_heads.transpose(1, 0, 2, 3).reshape(row_count, HEADS, HD)
    grad_keys = rotate(
        own_kv_grads[:, :kv_width].reshape(row_count, KV_HEADS, HD), places, -1.0
    ).reshape(row_count, kv_width)
    grad_project = jnp.concatenate(
        [
            rotate(grad_queries, places, -1.0).reshape(row_count, D),
            grad_keys,
            own_kv_grads[:, kv_width:],
        ],
        axis=1,
    ).astype(jnp.bfloat16)
    grad_normed = jnp.dot(grad_project, full_qkv.T, preferred_element_type=jnp.float32)
    grad_qkv = jnp.dot(normed.T, grad_project, preferred_element_type=jnp.float32)
    unused_first, norm_back_one = jax.vjp(normalize, inputs, gain_attn)
    grad_input_part, grad_gain_attn = norm_back_one(grad_normed)
    grad_inputs = grad_hidden + grad_input_part
    owned = (
        lax.psum_scatter(
            grad_gain_attn.astype(jnp.bfloat16), ("fsdp", "ctx"), scatter_dimension=0, tiled=True
        ).astype(jnp.float32),
        lax.psum_scatter(
            grad_gain_mlp.astype(jnp.bfloat16), ("fsdp", "ctx"), scatter_dimension=0, tiled=True
        ).astype(jnp.float32),
        lax.psum_scatter(
            grad_qkv.astype(jnp.bfloat16), ("fsdp", "ctx"), scatter_dimension=0, tiled=True
        ).astype(jnp.float32),
        lax.psum_scatter(
            grad_out_weight.astype(jnp.bfloat16), ("fsdp", "ctx"), scatter_dimension=0, tiled=True
        ).astype(jnp.float32),
        lax.psum_scatter(
            grad_gu.astype(jnp.bfloat16), ("fsdp", "ctx"), scatter_dimension=0, tiled=True
        ).astype(jnp.float32),
        lax.psum_scatter(
            grad_down.astype(jnp.bfloat16), ("fsdp", "ctx"), scatter_dimension=0, tiled=True
        ).astype(jnp.float32),
    )
    result_qkv, result_out, result_gu, result_down = (
        lax.psum_scatter(
            owned[2].astype(jnp.bfloat16), "dp", scatter_dimension=1, tiled=True
        ).astype(jnp.float32),
        lax.psum_scatter(
            owned[3].astype(jnp.bfloat16), "dp", scatter_dimension=1, tiled=True
        ).astype(jnp.float32),
        lax.psum_scatter(
            owned[4].astype(jnp.bfloat16), "dp", scatter_dimension=1, tiled=True
        ).astype(jnp.float32),
        lax.psum_scatter(
            owned[5].astype(jnp.bfloat16), "dp", scatter_dimension=1, tiled=True
        ).astype(jnp.float32),
    )
    gains_owned = (owned[0], owned[1])
    result_gain_attn, result_gain_mlp = lax.psum((gains_owned[0], gains_owned[1]), "dp")
    return (
        outputs[None],
        grad_inputs[None],
        result_gain_attn,
        result_gain_mlp,
        result_qkv,
        result_out,
        result_gu,
        result_down,
    )


def solution(mesh):
    placed = (
        P(("dp", "fsdp"), "ctx", None),
        P(("dp", "fsdp"), "ctx"),
        P(),
        P(),
        P("fsdp", None),
        P("fsdp", None),
        P("fsdp", None),
        P("fsdp", None),
        P(("dp", "fsdp"), "ctx", None),
    )
    return jax.shard_map(
        shards,
        mesh=mesh,
        in_specs=placed,
        out_specs=(
            P(("dp", "fsdp"), "ctx", None),
            P(("dp", "fsdp"), "ctx", None),
            P(("fsdp", "ctx")),
            P(("fsdp", "ctx")),
            P(("fsdp", "ctx"), "dp"),
            P(("fsdp", "ctx"), "dp"),
            P(("fsdp", "ctx"), "dp"),
            P(("fsdp", "ctx"), "dp"),
        ),
        check_vma=False,
    )
```

profile of v0, /device:TPU:0, one launch (start us, length us, event | category | flops | bytes accessed | tf_op | source)
XLA Modules:
  0.0 931.7 jit_solution(8227438307941456550)
XLA Ops:
  8.6 1.2 fusion.71
  10.0 46.9 %all-gather.6.cloned.1.call-done = bf16[960,1600]{1,0:T(8,128)(2,1)} async-done(((bf16[240,1600]{1,0:T(8,128)(2,1)}), bf16[960,1600]{1,0:T(8,128)(2,1)}) %all-gather.6.cloned.1.call-update) | async-done | bytes 3072016 | tf_op jit(solution)/shard_map/all_gather | solution.py:94
  57.0 3.7 fusion.80
  64.0 1.3 slice.79
  65.4 29.9 %all-gather.8.cloned.1.call-done = bf16[1024,640]{0,1:T(8,128)(2,1)} async-done(((bf16[256,640]{0,1:T(8,128)(2,1)}), bf16[1024,640]{0,1:T(8,128)(2,1)}) %all-gather.8.cloned.1.call-update) | async-done | bytes 1310736 | tf_op jit(solution)/shard_map/all_gather | solution.py:107
  95.3 1.4 fusion.90
  96.7 13.7 %while.30 = (s32[]{:T(128)}, bf16[5,256,3,64]{1,3,2,0:T(8,128)(2,1)S(1)}, f32[5,3,256,1]{2,1,3,0:T(4,128)S(1)}, f32[5,3,256,1]{2,1,3,0:T(4,128)S(1)}, bf16[5,102...) while((s32[]{:T(128)}, ...), condition=%wide.region_4.5_spmd.clone, body=%wide.region_1.4_spmd.sunk.clone | while | flops 211024640 | bytes 11080805 | solution.py:110
  110.5 19.5 %all-gather.10.cloned.1.call-done = bf16[960,960]{1,0:T(8,128)(2,1)} async-done(((bf16[240,960]{1,0:T(8,128)(2,1)}), bf16[960,960]{1,0:T(8,128)(2,1)}) %all-gather.10.cloned.1.call-update) | async-done | bytes 1843216 | tf_op jit(solution)/shard_map/all_gather | solution.py:95
  130.0 2.7 multiply_reduce_fusion.2
  132.7 98.6 %all-gather.12.cloned.1.call-done = bf16[960,5120]{1,0:T(8,128)(2,1)} async-done(((bf16[240,5120]{1,0:T(8,128)(2,1)}), bf16[960,5120]{1,0:T(8,128)(2,1)}) %all-gather.12.cloned.1.call-update) | async-done | bytes 9830416 | tf_op jit(solution)/shard_map/all_gather | solution.py:96
  231.3 8.7 fusion.88
  240.0 51.7 %all-gather.14.cloned.1.call-done = bf16[2560,960]{0,1:T(8,128)(2,1)} async-done(((bf16[640,960]{0,1:T(8,128)(2,1)}), bf16[2560,960]{0,1:T(8,128)(2,1)}) %all-gather.14.cloned.1.call-update) | async-done | bytes 4915216 | tf_op jit(solution)/shard_map/all_gather | solution.py:97
  291.7 8.0 fusion.60
  299.8 2.9 multiply_reduce_fusion
  303.0 1.2 copy-done.4
  304.9 43.9 %while.31 = (s32[]{:T(128)}, f32[5,256,3,64]{1,3,2,0:T(8,128)}, bf16[5,1024,64]{1,2,0:T(8,128)(2,1)}, bf16[5,1024,64]{1,2,0:T(8,128)(2,1)}, bf16[5,1024,64]{1,2,...) while((s32[]{:T(128)}, f32[5,256,3,64]{1,3,2,0:T(8,128)}, ...), condition=%wide.region_9.10_spmd.clone, body=%wide.region_7.9_spmd.sunk.clone | while | flops 511557120 | bytes 25658492 | solution.py:152
  305.1 1.5 fusion.155
  306.8 2.1 fusion.156
  309.4 1.1 fusion.158
  310.4 2.1 fusion.159
  312.6 1.3 fusion.160
  313.8 1.5 fusion.155
  315.6 2.1 fusion.156
  318.1 1.1 fusion.158
  319.2 2.1 fusion.159
  321.3 1.3 fusion.160
  322.6 1.5 fusion.155
  324.3 2.1 fusion.156
  327.9 2.1 fusion.159
  330.1 1.3 fusion.160
  331.3 1.5 fusion.155
  333.0 2.1 fusion.156
  335.6 1.1 fusion.158
  336.6 2.1 fusion.159
  338.8 1.3 fusion.160
  340.0 1.5 fusion.155
  341.8 2.1 fusion.156
  344.3 1.1 fusion.158
  345.4 2.1 fusion.159
  347.5 1.3 fusion.160
  348.8 2.6 pad_maximum_fusion.3
  351.4 5.0 convolution_convert_fusion.1
  356.5 1.2 copy-done.14
  358.7 2.0 convolution_convert_fusion.3
  360.7 5.4 convolution_convert_fusion
  366.1 16.6 %reduce-scatter.19.cloned.1.call-done = bf16[256,640]{0,1:T(8,128)(2,1)} async-done(((bf16[1024,640]{0,1:T(8,128)(2,1)}), bf16[256,640]{0,1:T(8,128)(2,1)}) %reduce-scatter.19.cloned.1.call-update) | async-done | bytes 327696 | tf_op jit(solution)/shard_map/reduce_scatter | solution.py:166
  384.6 2.8 convolution_convert_fusion.2
  387.4 435.1 %fusion.89 = (bf16[64,1600]{1,0:T(8,128)(2,1)S(1)}, bf16[64,960]{1,0:T(8,128)(2,1)S(1)}, bf16[64,5120]{1,0:T(8,128)(2,1)S(1)}) fusion(bf16[960,1600]{1,0:T(8,128)(2,1)} %convolution_convert_fusion.2, bf16[960,960]{1,0:T(8,128)(2,1)} %convolution_convert_fusion.3, bf16[960,5120]{1,0:T(8,128)(2,1)} %convolution_convert_fusion), kind=kCustom, calls=%all-reduce-scatter.3 | all-reduce-scatter fusion | flops 7864321 | bytes 15729152
  823.4 2.1 collective-permute-start.2
  826.3 1.9 collective-permute-start.1
  828.9 2.0 collective-permute-start
  832.2 10.8 %collective-permute-done.1 = bf16[60,960]{1,0:T(8,128)(2,1)} collective-permute-done((bf16[60,960]{1,0:T(8,128)(2,1)}, bf16[60,960]{1,0:T(8,128)(2,1)}, u32[]{:S(2)}, u32[]{:S(2)}) %collective-permute-start.1) | collective-permute-done | bytes 115232
  843.0 3.0 concatenate.47
  847.9 3.8 concatenate.46
  853.8 8.1 concatenate.48
  861.9 2.1 constant_dynamic-slice_fusion
  865.0 5.4 fusion.63
  870.4 1.2 fusion.67
  871.6 40.1 %all-reduce.9 = (bf16[960]{0:T(1024)(128)(2,1)S(1)}, bf16[960]{0:T(1024)(128)(2,1)S(1)}) all-reduce(bf16[960]{0:T(1024)(128)(2,1)S(1)} %get-tuple-element.119, bf16[960]{0:T(1024)(128)(2,1)S(1)} %get-tuple-element.117), channel_id=3, replica_groups=mesh['dp'=2,'fsdp'=4,'ctx'=4] {'fsdp','ctx'}, use_global_device_ids=true, to_apply=%region_13.14.clone | all-reduce | flops 1920 | bytes 7680
  911.7 2.0 copy.33
  913.8 3.0 all-reduce.8
  916.8 1.2 fusion.70
  919.7 1.1 copy.30
  921.5 1.9 convert_element_type.135
  (170 shorter events, 38.4 us)
Async XLA Ops:
  7.2 49.8 %all-gather.6.cloned.1.call-start = ((), (), s32[]{:S(2)}) async-start(), calls=%async_computation.6 | async-start | bytes 3993600 | tf_op jit(solution)/shard_map/all_gather | solution.py:94
  7.9 87.4 %all-gather.8.cloned.1.call-start = ((), (), s32[]{:S(2)}) async-start(), calls=%async_computation.7 | async-start | bytes 1638400 | tf_op jit(solution)/shard_map/all_gather | solution.py:107
  60.6 2.4 copy-start.9
  61.7 68.2 %all-gather.10.cloned.1.call-start = ((), (), s32[]{:S(2)}) async-start(), calls=%async_computation.8 | async-start | bytes 2457600 | tf_op jit(solution)/shard_map/all_gather | solution.py:95
  62.5 168.8 %all-gather.12.cloned.1.call-start = ((), (), s32[]{:S(2)}) async-start(), calls=%async_computation.9 | async-start | bytes 12288000 | tf_op jit(solution)/shard_map/all_gather | solution.py:96
  63.0 228.7 %all-gather.14.cloned.1.call-start = ((), (), s32[]{:S(2)}) async-start(), calls=%async_computation.10 | async-start | bytes 6144000 | tf_op jit(solution)/shard_map/all_gather | solution.py:97
  63.6 319.1 %reduce-scatter.19.cloned.1.call-start = ((), (), s32[]{:S(2)}) async-start(), calls=%async_computation.11 | async-start | bytes 1638400 | tf_op jit(solution)/shard_map/reduce_scatter | solution.py:166
  110.4 19.5 %copy-start.7 = (bf16[5,256,3,64]{1,3,2,0:T(8,128)(2,1)}, bf16[5,256,3,64]{1,3,2,0:T(8,128)(2,1)S(1)}, u32[]{:S(2)}) copy-start(bf16[5,256,3,64]{1,3,2,0:T(8,128)(2,1)S(1)} %get-tuple-element.111) | copy-start | bytes 1474564
  110.4 129.6 %copy-start.2 = (bf16[5,1024,64]{1,2,0:T(8,128)(2,1)}, bf16[5,1024,64]{1,2,0:T(8,128)(2,1)S(1)}, u32[]{:S(2)}) copy-start(bf16[5,1024,64]{1,2,0:T(8,128)(2,1)S(1)} %get-tuple-element.459) | copy-start | bytes 1966084
  110.4 129.6 %copy-start.3 = (bf16[5,256,3,64]{1,3,2,0:T(8,128)(2,1)}, bf16[5,256,3,64]{1,3,2,0:T(8,128)(2,1)S(1)}, u32[]{:S(2)}) copy-start(bf16[5,256,3,64]{1,3,2,0:T(8,128)(2,1)S(1)} %get-tuple-element.464) | copy-start | bytes 1474564
  110.5 120.8 %copy-start.15 = (f32[960]{0:T(1024)S(1)}, f32[960]{0:T(1024)}, u32[]{:S(2)}) copy-start(f32[960]{0:T(1024)} %param.16) | copy-start | bytes 11524
  291.7 8.0 copy-start
  299.7 2.9 copy-start.10
  299.7 2.9 copy-start.12
  299.7 2.9 copy-start.5
  302.6 1.5 copy-start.4
  348.8 2.7 copy-start.1
  351.4 560.4 %reduce-scatter.23.cloned.1.call-start = ((), (), s32[]{:S(2)}) async-start(), calls=%async_computation.13 | async-start | bytes 5570560 | tf_op jit(solution)/shard_map/reduce_scatter | solution.py:202
  356.4 1.3 copy-start.14
  356.4 2.3 copy-start.8
  356.5 561.5 %reduce-scatter.27.cloned.1.call-start = ((), (), s32[]{:S(2)}) async-start(), calls=%async_computation.15 | async-start | bytes 368640
  357.7 2.9 copy-start.11
  357.7 2.9 copy-start.13
  360.7 23.9 %copy-start.6 = (bf16[1,256,960]{1,2,0:T(8,128)(2,1)S(1)}, bf16[1,256,960]{1,2,0:T(8,128)(2,1)}, u32[]{:S(2)}) copy-start(bf16[1,256,960]{1,2,0:T(8,128)(2,1)} %param.13) | copy-start | bytes 1474564
  360.7 23.9 %copy-start.16 = (bf16[256,15,64]{0,2,1:T(8,128)(2,1)S(1)}, bf16[256,15,64]{0,2,1:T(8,128)(2,1)}, u32[]{:S(2)}) copy-start(bf16[256,15,64]{0,2,1:T(8,128)(2,1)} %pad_maximum_fusion.5) | copy-start | bytes 1474564
  360.7 23.9 %copy-start.22 = (f32[960]{0:T(1024)S(1)}, f32[960]{0:T(1024)}, u32[]{:S(2)}) copy-start(f32[960]{0:T(1024)} %param.15) | copy-start | bytes 11524
  383.8 0.7 copy-start.18
  383.9 0.7 copy-start.20
  387.4 443.6 %copy-start.23 = (u32[32]{0:T(128)S(1)}, u32[32]{0:T(128)}, u32[]{:S(2)}) copy-start(u32[32]{0:T(128)} %constant.87) | copy-start | bytes 388
  823.4 30.4 %collective-permute-start.2 = (bf16[60,5120]{1,0:T(8,128)(2,1)}, bf16[60,5120]{1,0:T(8,128)(2,1)}, u32[]{:S(2)}, u32[]{:S(2)}) collective-permute-start(bf16[60,5120]{1,0:T(8,128)(2,1)} %slice.92), channel_id=1, source_target_pairs={{0,1},{1,2},{2,3},{3,4},{4,5},{5,6},{6,7},{7,8},{8,9},{9,10},{10,1... | collective-permute-start | bytes 1843208
  826.3 16.7 %collective-permute-start.1 = (bf16[60,960]{1,0:T(8,128)(2,1)}, bf16[60,960]{1,0:T(8,128)(2,1)}, u32[]{:S(2)}, u32[]{:S(2)}) collective-permute-start(bf16[60,960]{1,0:T(8,128)(2,1)} %slice.91), channel_id=1, source_target_pairs={{0,1},{1,2},{2,3},{3,4},{4,5},{5,6},{6,7},{7,8},{8,9},{9,10},{10,1... | collective-permute-start | bytes 345608
  828.9 19.0 %collective-permute-start = (bf16[60,1600]{1,0:T(8,128)(2,1)}, bf16[60,1600]{1,0:T(8,128)(2,1)}, u32[]{:S(2)}, u32[]{:S(2)}) collective-permute-start(bf16[60,1600]{1,0:T(8,128)(2,1)} %slice.90), channel_id=1, source_target_pairs={{0,1},{1,2},{2,3},{3,4},{4,5},{5,6},{6,7},{7,8},{8,9},{9,10},{10,1... | collective-permute-start | bytes 576008
  847.9 71.8 %reduce-scatter.25.cloned.1.call-start = ((), (), s32[]{:S(2)}) async-start(), calls=%async_computation.14 | async-start | bytes 614400
  853.7 67.7 %reduce-scatter.21.cloned.1.call-start = ((), (), s32[]{:S(2)}) async-start(), calls=%async_computation.12 | async-start | bytes 983040 | tf_op jit(solution)/shard_map/reduce_scatter | solution.py:213
  864.0 59.3 %reduce-scatter.29.cloned.1.call-start = ((), (), s32[]{:S(2)}) async-start(), calls=%async_computation.16 | async-start | bytes 737280
  865.0 5.4 copy-start.17
  865.0 5.4 copy-start.19
  865.0 5.4 copy-start.21
  865.0 5.4 copy-start.24
Sparse Core Ops, SparseCore 0:
  9.8 47.0 all-gather.5
  61.8 33.4 all-gather.7
  97.2 32.7 all-gather.9
  131.6 99.5 all-gather.11
  233.0 58.6 all-gather.13
  351.5 31.2 reduce-scatter.18
  385.0 219.8 reduce-scatter.22
  848.0 10.6 reduce-scatter.26
  860.9 8.9 reduce-scatter.24
  872.7 9.2 reduce-scatter.20
  913.8 9.0 reduce-scatter.28
where the time goes:
time: 935 us; the launch traced here: 932 us
  blocking collectives  478 us (51%)
  waiting for transfers between devices  277 us (30%)
  matrix products  97.5 us (10%)
  local copies, waits for them, and re-layouts  36 us (4%)
  other arithmetic  20.3 us (2%)
  between operations  15.6 us (2%)
    unnamed x2, blocking collectives  475 us
    all_gather x1, waiting for transfers between devices, shards(): lax.all_gather(w_gu, 'fsdp', axis=0, tiled=True)  98.6 us
    all_gather x1, waiting for transfers between devices, shards(): lax.all_gather(w_down, 'fsdp', axis=0, tiled=True)  51.7 us
    all_gather x1, waiting for transfers between devices, shards(): lax.all_gather(w_qkv, 'fsdp', axis=0, tiled=True)  46.9 us
    unnamed x66, local copies, waits for them, and re-layouts  32.1 us
    all_gather x1, waiting for transfers between devices, shards(): every_kv = lax.all_gather(local_kv, 'ctx', axis=0, tiled=True)  29.9 us
    all_gather x1, waiting for transfers between devices, shards(): lax.all_gather(w_out, 'fsdp', axis=0, tiled=True)  19.5 us
  transfers between devices with their start and end apart: 14, of which 7 were waited for; matrix products, arithmetic and copies ran while one was open for 56% of the time, Pallas kernels for 0%

commit v1 on v0

v1 whole, which is shorter than its diff:
```python
import jax
import jax.numpy as jnp
from jax import lax
from jax.experimental import pallas as pl
from jax.experimental.pallas import tpu as pltpu
from jax.sharding import PartitionSpec as P

D = 960
HEADS = 15
KV_HEADS = 5
HD = 64
FF = 2560
GROUP = HEADS // KV_HEADS
KVW = KV_HEADS * HD
EPSILON = 1e-05
F32 = jnp.float32
BF16 = jnp.bfloat16


def dot(a, b, ca, cb):
    return lax.dot_general(a, b, (((ca,), (cb,)), ((), ())), preferred_element_type=F32)


def normalize(values, gain):
    return values * lax.rsqrt(jnp.mean(values * values, axis=-1, keepdims=True) + EPSILON) * gain


def angles_of(places):
    half = HD // 2
    frequency = 10000.0 ** (-jnp.arange(half, dtype=F32) / half)
    angles = frequency[:, None] * places.astype(F32)[None, :]
    return jnp.cos(angles), jnp.sin(angles)


def rotate(values, cosine, sine):
    length = values.shape[1]
    parts = values.reshape(-1, 2, HD // 2, length)
    front, back = parts[:, 0], parts[:, 1]
    turned = jnp.stack([front * cosine - back * sine, back * cosine + front * sine], axis=1)
    return turned.reshape(-1, length)


def keys_first(kv, which):
    pieces = [kv[c, which] for c in range(kv.shape[0])]
    return (
        jnp.concatenate([piece.T for piece in pieces], axis=0),
        jnp.concatenate(pieces, axis=1),
    )


def allowed_of(keys, rows):
    start = lax.axis_index("ctx") * rows
    key_at = lax.broadcasted_iota(jnp.int32, (keys, rows), 0)
    row_at = lax.broadcasted_iota(jnp.int32, (keys, rows), 1)
    return key_at <= row_at + start


def forward_kernel(q_ref, kv_ref, att_ref, lse_ref):
    rows = q_ref.shape[1]
    kv = kv_ref[...]
    keys, _ = keys_first(kv, 0)
    values_t = jnp.concatenate([kv[c, 1] for c in range(kv.shape[0])], axis=1)
    allowed = allowed_of(keys.shape[0], rows)
    for h in range(GROUP):
        q = q_ref[h * HD : (h + 1) * HD, :]
        scores = jnp.where(allowed, dot(keys, q, 1, 0), -1e30)
        row_max = jnp.max(scores, axis=0, keepdims=True)
        exponent = jnp.exp(scores - row_max)
        total = jnp.sum(exponent, axis=0, keepdims=True)
        att = dot(values_t, exponent.astype(BF16), 1, 0) / total
        att_ref[h * HD : (h + 1) * HD, :] = att.astype(BF16)
        lse_ref[0, h : h + 1, :] = row_max + jnp.log(total)


def backward_kernel(q_ref, kv_ref, g_ref, lse_ref, dq_ref, dkv_ref):
    rows = q_ref.shape[1]
    kv = kv_ref[...]
    parts = kv.shape[0]
    keys, keys_t = keys_first(kv, 0)
    values, _ = keys_first(kv, 1)
    allowed = allowed_of(keys.shape[0], rows)
    dk = jnp.zeros((HD, keys.shape[0]), F32)
    dv = jnp.zeros((HD, keys.shape[0]), F32)
    for h in range(GROUP):
        q = q_ref[h * HD : (h + 1) * HD, :]
        g = g_ref[h * HD : (h + 1) * HD, :]
        scores = jnp.where(allowed, dot(keys, q, 1, 0), -1e30)
        prob = jnp.exp(scores - lse_ref[0, h : h + 1, :])
        dprob = dot(values, g, 1, 0)
        inner = jnp.sum(dprob * prob, axis=0, keepdims=True)
        ds = (prob * (dprob - inner)).astype(BF16)
        dq_ref[h * HD : (h + 1) * HD, :] = dot(keys_t, ds, 1, 0) * (HD**-0.5)
        dk = dk + dot(q, ds, 1, 1)
        dv = dv + dot(g, prob.astype(BF16), 1, 1)
    for c in range(parts):
        dkv_ref[c, 0] = dk[:, c * rows : (c + 1) * rows].astype(BF16)
        dkv_ref[c, 1] = dv[:, c * rows : (c + 1) * rows].astype(BF16)


def attention_specs(parts, rows):
    q_spec = pl.BlockSpec((GROUP * HD, rows), lambda g: (g, 0))
    kv_spec = pl.BlockSpec((parts, 2, HD, rows), lambda g: (0, 0, g, 0))
    lse_spec = pl.BlockSpec((1, GROUP, rows), lambda g: (g, 0, 0))
    return q_spec, kv_spec, lse_spec


def attention_forward(q, kv):
    parts, rows = kv.shape[0], q.shape[1]
    q_spec, kv_spec, lse_spec = attention_specs(parts, rows)
    work = parts * rows * rows * HD * HEADS
    return pl.pallas_call(
        forward_kernel,
        grid=(KV_HEADS,),
        in_specs=[q_spec, kv_spec],
        out_specs=[q_spec, lse_spec],
        out_shape=[
            jax.ShapeDtypeStruct((D, rows), BF16),
            jax.ShapeDtypeStruct((KV_HEADS, GROUP, rows), F32),
        ],
        compiler_params=pltpu.CompilerParams(vmem_limit_bytes=40 * 2**20),
        cost_estimate=pl.CostEstimate(
            flops=16 * work, bytes_accessed=3 * 2**20, transcendentals=work // HD
        ),
    )(q, kv)


def attention_backward(q, kv, g, lse):
    parts, rows = kv.shape[0], q.shape[1]
    q_spec, kv_spec, lse_spec = attention_specs(parts, rows)
    work = parts * rows * rows * HD * HEADS
    return pl.pallas_call(
        backward_kernel,
        grid=(KV_HEADS,),
        in_specs=[q_spec, kv_spec, q_spec, lse_spec],
        out_specs=[q_spec, kv_spec],
        out_shape=[
            jax.ShapeDtypeStruct((D, rows), F32),
            jax.ShapeDtypeStruct(kv.shape, BF16),
        ],
        compiler_params=pltpu.CompilerParams(vmem_limit_bytes=40 * 2**20),
        cost_estimate=pl.CostEstimate(
            flops=40 * work, bytes_accessed=5 * 2**20, transcendentals=work // HD
        ),
    )(q, kv, g, lse)


def halves(grad, dp):
    rows, columns = grad.shape
    return grad.reshape(rows, dp, columns // dp).transpose(1, 0, 2)


def over_dp(grad):
    return lax.psum_scatter(grad, "dp", scatter_dimension=0, tiled=True)


def shards(tokens, positions, gain_attn, gain_mlp, w_qkv, w_out, w_gu, w_down, cotangent):
    rows = tokens.shape[1]
    fsdp, ctx, dp = lax.axis_size("fsdp"), lax.axis_size("ctx"), lax.axis_size("dp")
    part = FF // fsdp
    own = D // fsdp
    slim = D // (fsdp * ctx)
    inputs = tokens[0].astype(F32)
    cosine, sine = angles_of(positions[0])
    full_qkv = lax.all_gather(w_qkv, "fsdp", axis=0, tiled=True)
    full_out = lax.all_gather(w_out, "fsdp", axis=0, tiled=True)
    cot_all = lax.all_gather(cotangent[0], "fsdp", axis=0, tiled=True)
    gu_cut = w_gu.reshape(own, 2, fsdp, part).transpose(2, 0, 1, 3).reshape(fsdp, own, 2 * part)
    gu_part = lax.all_to_all(gu_cut, "fsdp", 0, 0).reshape(D, 2 * part)

    normed = normalize(inputs, gain_attn).astype(BF16)
    project = dot(full_qkv, normed, 0, 1)
    turned = rotate(project[: D + KVW], cosine, sine)
    queries = (turned[:D] * (HD**-0.5)).astype(BF16)
    local_kv = jnp.concatenate([turned[D:].astype(BF16), project[D + KVW :].astype(BF16)], axis=0)
    every_kv = lax.all_gather(local_kv, "ctx", axis=0, tiled=False).reshape(ctx, 2, KVW, rows)
    attended, lse = attention_forward(queries, every_kv)
    hidden = inputs + dot(attended, full_out, 0, 0)
    normed_two = normalize(hidden, gain_mlp).astype(BF16)

    two_all = lax.all_gather(normed_two, "fsdp", axis=0, tiled=True)
    gate_up = dot(two_all, gu_part, 1, 0)
    gate, up = gate_up[:, :part], gate_up[:, part:]
    activated, swish_back = jax.vjp(lambda a, b: jax.nn.silu(a) * b, gate, up)
    activated = activated.astype(BF16)
    grad_activated = dot(cot_all, w_down, 1, 1)
    grad_gate, grad_up = swish_back(grad_activated)
    grad_gate_up = jnp.concatenate([grad_gate, grad_up], axis=1).astype(BF16)
    two_part = dot(grad_gate_up, gu_part, 1, 1).astype(BF16)
    grad_two = lax.psum_scatter(two_part, "fsdp", scatter_dimension=0, tiled=True).astype(F32)
    down_part = dot(activated, w_down, 1, 0).astype(BF16)
    down_sum = lax.psum_scatter(down_part, "fsdp", scatter_dimension=0, tiled=True)
    outputs = hidden + down_sum.astype(F32)
    grad_down = dot(activated, cot_all, 0, 0).astype(BF16)
    grad_gu = dot(two_all, grad_gate_up, 0, 0).astype(BF16)

    result_down = lax.psum_scatter(
        over_dp(halves(grad_down, dp)).reshape(ctx, part // ctx, D // dp),
        "ctx",
        scatter_dimension=0,
        tiled=True,
    )[0]
    if dp == 2:
        gu_cols = over_dp(halves(grad_gu, dp))[0]
    else:
        gu_cols = grad_gu
    gu_rows = lax.psum_scatter(
        gu_cols.reshape(fsdp, ctx, slim, -1).transpose(1, 0, 2, 3),
        "ctx",
        scatter_dimension=0,
        tiled=True,
    )[0]
    gu_rows = lax.all_to_all(gu_rows, "fsdp", 0, 0)
    if dp == 2:
        result_gu = gu_rows.transpose(1, 0, 2).reshape(slim, FF)
    else:
        gu_rows = gu_rows.reshape(fsdp, slim, 2, part).transpose(1, 2, 0, 3).reshape(slim, 2 * FF)
        result_gu = lax.psum_scatter(gu_rows, "dp", scatter_dimension=1, tiled=True)

    grad_rows = cotangent[0].astype(F32)
    _, norm_back_two = jax.vjp(normalize, hidden, gain_mlp)
    grad_hidden_part, grad_gain_mlp = norm_back_two(grad_two)
    grad_hidden = grad_rows + grad_hidden_part
    grad_attn = grad_hidden.astype(BF16)
    grad_attended = dot(full_out, grad_attn, 1, 1).astype(BF16)
    grad_out = dot(attended, grad_attn, 1, 0).astype(BF16)
    grad_queries, kv_grads = attention_backward(queries, every_kv, grad_attended, lse)
    own_kv = lax.psum_scatter(
        kv_grads.reshape(ctx, 2 * KVW, rows), "ctx", scatter_dimension=0, tiled=True
    )[0].astype(F32)
    grad_project = jnp.concatenate(
        [
            rotate(grad_queries, cosine, -sine),
            rotate(own_kv[:KVW], cosine, -sine),
            own_kv[KVW:],
        ],
        axis=0,
    ).astype(BF16)
    grad_normed = dot(grad_project, full_qkv, 0, 1)
    grad_qkv = dot(normed, grad_project, 0, 1).astype(BF16)
    _, norm_back_one = jax.vjp(normalize, inputs, gain_attn)
    grad_input_part, grad_gain_attn = norm_back_one(grad_normed)
    grad_inputs = grad_hidden + grad_input_part

    both = over_dp(jnp.concatenate([halves(grad_qkv, dp), halves(grad_out, dp)], axis=2))
    both = lax.psum_scatter(
        both.reshape(fsdp * ctx, slim, -1), ("fsdp", "ctx"), scatter_dimension=0, tiled=True
    )[0]
    wide = w_qkv.shape[1] // dp
    gains = lax.psum(jnp.stack([grad_gain_attn, grad_gain_mlp]), ("dp", "fsdp", "ctx"))
    place = lax.axis_index("fsdp") * ctx + lax.axis_index("ctx")
    gains = lax.dynamic_slice(gains, (0, place * slim), (2, slim))
    return (
        outputs[None],
        grad_inputs[None],
        gains[0],
        gains[1],
        both[:, :wide].astype(F32),
        both[:, wide:].astype(F32),
        result_gu.astype(F32),
        result_down.astype(F32),
    )


def solution(mesh):
    placed = (
        P(("dp", "fsdp"), "ctx", None),
        P(("dp", "fsdp"), "ctx"),
        P(),
        P(),
        P("fsdp", None),
        P("fsdp", None),
        P("fsdp", None),
        P("fsdp", None),
        P(("dp", "fsdp"), "ctx", None),
    )
    return jax.shard_map(
        shards,
        mesh=mesh,
        in_specs=placed,
        out_specs=(
            P(("dp", "fsdp"), "ctx", None),
            P(("dp", "fsdp"), "ctx", None),
            P(("fsdp", "ctx")),
            P(("fsdp", "ctx")),
            P(("fsdp", "ctx"), "dp"),
            P(("fsdp", "ctx"), "dp"),
            P(("fsdp", "ctx"), "dp"),
            P(("fsdp", "ctx"), "dp"),
        ),
        check_vma=False,
    )
```

time: 935 us -> 583 us (0.62)
  blocking collectives: 478 us -> 82.5 us
  waiting for transfers between devices: 277 us -> 332 us
  matrix products: 97.5 us -> 46.5 us
  Pallas kernels: 0 us -> 27.6 us
  local copies, waits for them, and re-layouts: 36 us -> 50.6 us
    unnamed x2 -> x0, blocking collectives: 475 us -> none
    reduce_scatter x3 -> x8, waiting for transfers between devices: 16.6 us -> 159 us  [the longest x1 39 us: shards(): lax.psum_scatter(both.reshape(fsdp * ctx, slim, -1), ('fsdp', 'ctx'), sca...]
    all_gather x5, waiting for transfers between devices: 247 us -> 119 us  [the longest x1 46.9 us: shards(): full_qkv = lax.all_gather(w_qkv, 'fsdp', axis=0, tiled=True)]
    dot_general x47 -> x12, matrix products: 97.5 us -> 46.5 us  [dot(): lax.dot_general(a, b, (((ca,), (cb,)), ((), ())), preferred_element_type=...]
    all_to_all x0 -> x1, blocking collectives: none -> 43 us  [shards(): gu_part = lax.all_to_all(gu_cut, 'fsdp', 0, 0).reshape(D, 2 * part)]
    unnamed x17 -> x15, waiting for transfers between devices: 13.4 us -> 53.6 us
    psum x1, blocking collectives: 2.95 us -> 39.4 us  [shards(): lax.psum(jnp.stack([grad_gain_attn, grad_gain_mlp]), ('dp', 'fsdp', 'ctx'))]
    pallas_call x0 -> x2, Pallas kernels: none -> 27.6 us  [the longest x1 16.5 us: attention_backward(): pl.pallas_call(backward_kernel, grid=(KV_HEADS,), in_specs=[q_spec, kv_sp...]
  transfers between devices with their start and end apart: 14 -> 15, of which waited for: 7 -> 12; matrix products, arithmetic and copies ran while one was open for 56% -> 15% of each run, Pallas kernels for 0% -> 2%
where the time goes in v1:
time: 583 us; the launch traced here: 582 us
  waiting for transfers between devices  332 us (57%)
  blocking collectives  82.5 us (14%)
  local copies, waits for them, and re-layouts  50.6 us (9%)
  matrix products  46.5 us (8%)
  Pallas kernels  27.6 us (5%)
  other arithmetic  23.4 us (4%)
  between operations  14.3 us (2%)
    unnamed x15, waiting for transfers between devices  53.6 us
    all_gather x1, waiting for transfers between devices, shards(): full_qkv = lax.all_gather(w_qkv, 'fsdp', axis=0, tiled=True)  46.9 us
    dot_general x12, matrix products, dot(): lax.dot_general(a, b, (((ca,), (cb,)), ((), ())), preferred_element_type=...  46.5 us
    all_to_all x1, blocking collectives, shards(): gu_part = lax.all_to_all(gu_cut, 'fsdp', 0, 0).reshape(D, 2 * part)  43 us
    psum x1, blocking collectives, shards(): lax.psum(jnp.stack([grad_gain_attn, grad_gain_mlp]), ('dp', 'fsdp', 'ctx'))  39.4 us
    reduce_scatter x1, waiting for transfers between devices, shards(): lax.psum_scatter(both.reshape(fsdp * ctx, slim, -1), ('fsdp', 'ctx'), sca...  39 us
    reduce_scatter x1, waiting for transfers between devices, shards(): lax.psum_scatter(down_part, 'fsdp', scatter_dimension=0, tiled=True)  35.7 us
    all_gather x1, waiting for transfers between devices, shards(): lax.all_gather(local_kv, 'ctx', axis=0, tiled=False)  30.9 us
  transfers between devices with their start and end apart: 15, of which 12 were waited for; matrix products, arithmetic and copies ran while one was open for 15% of the time, Pallas kernels for 2%

profile of v1, /device:TPU:0, one launch (start us, length us, event | category | flops | bytes accessed | tf_op | source)
XLA Modules:
  0.0 581.7 jit_solution(2620770695809298398)
XLA Ops:
  7.2 0.7 all-gather.8.cloned.1.call-update
  8.0 0.7 convert_element_type.94
  8.7 1.2 fusion.26
  10.1 46.9 %all-gather.8.cloned.1.call-done = bf16[960,1600]{1,0:T(8,128)(2,1)} async-done(((bf16[240,1600]{1,0:T(8,128)(2,1)}), bf16[960,1600]{1,0:T(8,128)(2,1)}) %all-gather.8.cloned.1.call-update) | async-done | bytes 3072016 | tf_op jit(solution)/shard_map/all_gather | solution.py:164
  57.0 3.7 convolution_bitcast_fusion
  61.0 0.8 copy-done.5
  61.9 0.7 pad_maximum_fusion.9
  62.7 0.7 all-gather.10.cloned.1.call-update
  63.4 1.1 fusion.22
  64.6 30.9 %all-gather.14.cloned.1.call-done = bf16[2560,256]{1,0:T(8,128)(2,1)} async-done(((bf16[640,256]{1,0:T(8,128)(2,1)}), bf16[2560,256]{1,0:T(8,128)(2,1)}) %all-gather.14.cloned.1.call-update) | async-done | bytes 1310736 | tf_op jit(solution)/shard_map/all_gather | solution.py:175
  95.5 1.3 copy-done.2
  96.8 11.1 %shard_map.152 = (bf16[960,256]{1,0:T(8,128)(2,1)S(1)}, f32[5,3,256]{2,1,0:T(4,128)S(1)}) custom-call(bf16[960,256]{1,0:T(8,128)(2,1)S(1)} %bitcast.98, bf16[4,2,320,256]{3,2,1,0:T(8,128)(2,1)S(1)} %bitcast.100), custom_call_target="tpu_custom_call" | custom-call | flops 4026531840 | bytes 3145728 | tf_op jit(solution)/shard_map/pallas_call | solution.py:111
  107.9 22.7 %all-gather.10.cloned.1.call-done = bf16[960,960]{1,0:T(8,128)(2,1)} async-done(((bf16[240,960]{1,0:T(8,128)(2,1)}), bf16[960,960]{1,0:T(8,128)(2,1)}) %all-gather.10.cloned.1.call-update) | async-done | bytes 1843216 | tf_op jit(solution)/shard_map/all_gather | solution.py:165
  130.6 2.5 multiply_reduce_fusion
  133.2 1.1 multiply_convert_fusion.2
  134.9 5.6 reshape.228
  140.5 5.2 copy.61
  145.7 6.6 %reshape.229 = bf16[4,240,1280]{2,1,0:T(8,128)(2,1)} reshape(bf16[4,240,2,640]{3,2,1,0:T(2,128)(2,1)} %bitcast.104) | data formatting | bytes 4915200 | tf_op jit(solution)/shard_map/reshape | solution.py:167
  152.3 43.0 %all_to_all.10 = bf16[4,240,1280]{2,1,0:T(8,128)(2,1)} all-to-all(bf16[4,240,1280]{2,1,0:T(8,128)(2,1)} %reshape.229), channel_id=1, replica_groups=mesh['dp'=2,'fsdp'=4,'ctx'=4] {'fsdp'}, dimensions={0} | all-to-all | bytes 4915200 | tf_op jit(solution)/shard_map/all_to_all | solution.py:168
  195.4 7.7 %fusion.42 = f32[1024,1280]{1,0:T(8,128)} fusion(bf16[1024,960]{0,1:T(8,128)(2,1)} %all-gather.12.cloned.1.call-done, bf16[960,1280]{1,0:T(8,128)(2,1)} %bitcast.110), kind=kOutput, calls=%fused_computation.96 | convolution fusion | flops 2516582400 | bytes 9666560 | tf_op jit(solution)/shard_map/dot_general | solution.py:21
  203.1 18.8 %all-gather.16.cloned.1.call-done = bf16[1,1024,960]{1,2,0:T(8,128)(2,1)} async-done(((bf16[1,256,960]{1,2,0:T(8,128)(2,1)}), bf16[1,1024,960]{1,2,0:T(8,128)(2,1)}) %all-gather.16.cloned.1.call-update) | async-done | bytes 1966096 | tf_op jit(solution)/shard_map/all_gather | solution.py:166
  221.9 7.1 %fusion.2 = (bf16[1024,640]{1,0:T(8,128)(2,1)S(1)}, bf16[1024,640]{1,0:T(8,128)(2,1)S(1)}, bf16[1024,640]{1,0:T(8,128)(2,1)}) fusion(f32[1024,1280]{1,0:T(8,128)} %fusion.42, bf16[640,960]{0,1:T(8,128)(2,1)S(1)} %copy-done, bf16[1,1024,960]{1,2,0:T(8,128)(2,1)} %all-gather.16.cloned.1.call-done), kind=kOutput, calls=%fused_computation.7 | convolution fusion | flops 1268776960 | bytes 12369920 | tf_op jit(solution)/shard_map/dot_general | solution.py:21
  229.0 1.1 copy-done.21
  230.6 4.0 convolution_convert_fusion.2
  234.6 4.3 convolution_convert_fusion.4
  239.0 29.8 %reduce-scatter.11.cloned.1.call-done = bf16[256,960]{0,1:T(8,128)(2,1)} async-done(((bf16[1024,960]{0,1:T(8,128)(2,1)}), bf16[256,960]{0,1:T(8,128)(2,1)}) %reduce-scatter.11.cloned.1.call-update) | async-done | bytes 491536 | tf_op jit(solution)/shard_map/reduce_scatter | solution.py:189
  268.9 1.5 fusion.19
  270.4 35.7 %reduce-scatter.9.cloned.1.call-done = bf16[256,960]{0,1:T(8,128)(2,1)} async-done(((bf16[1024,960]{0,1:T(8,128)(2,1)}), bf16[256,960]{0,1:T(8,128)(2,1)}) %reduce-scatter.9.cloned.1.call-update) | async-done | bytes 491536 | tf_op jit(solution)/shard_map/reduce_scatter | solution.py:191
  306.0 2.9 fusion.23
  309.0 0.7 fusion.11.g_ref
  309.7 0.6 copy-done.3
  310.3 16.5 %shard_map.153 = (f32[960,256]{1,0:T(8,128)S(1)}, bf16[4,2,320,256]{3,2,1,0:T(8,128)(2,1)}) custom-call(bf16[960,256]{1,0:T(8,128)(2,1)S(1)} %bitcast.99, bf16[4,2,320,256]{3,2,1,0:T(8,128)(2,1)S(1)} %bitcast.101, bf16[960,256]{1,0:T(8,128)(2,1)S(1)} %fusion.11.g_ref, f32[5,3,256]{2,1,0:T(4,128)S(1)} %get-tuple-element.13.lse_ref), custom_call_target="tpu_custom_call" | custom-call | flops 10066329600 | bytes 5242880 | tf_op jit(solution)/shard_map/pallas_call | solution.py:131
  327.1 5.0 convolution_convert_fusion
  332.1 1.7 copy.60
  333.9 4.6 fusion.8
  338.8 2.0 convolution_convert_fusion.3
  340.8 17.4 %reduce-scatter.13.cloned.1.call-done = bf16[1,640,256]{2,1,0:T(8,128)(2,1)} async-done(((bf16[4,640,256]{2,1,0:T(8,128)(2,1)}), bf16[1,640,256]{2,1,0:T(8,128)(2,1)}) %reduce-scatter.13.cloned.1.call-update) | async-done | bytes 327696 | tf_op jit(solution)/shard_map/reduce_scatter | solution.py:227
  358.2 1.0 fusion.41
  359.4 2.8 convolution_convert_fusion.1
  362.2 5.5 copy.48
  367.7 5.9 %pad_maximum_fusion = bf16[2,960,1280]{1,2,0:T(8,128)(2,1)} fusion(bf16[2,960,480]{1,2,0:T(8,128)(2,1)} %bitcast.105, bf16[2,960,800]{1,2,0:T(8,128)(2,1)} %bitcast.102), kind=kLoop, calls=%fused_computation | loop fusion | flops 9830400 | bytes 9830400 | tf_op jit(solution)/shard_map/concatenate | solution.py:244
  373.7 1.4 reshape_squeeze.3
  375.1 2.0 copy.51
  377.1 4.3 reduce-scatter.21.cloned.1.call-done
  381.4 2.1 copy.54
  383.6 14.6 %reduce-scatter.15.cloned.1.call-done = bf16[1,960,1280]{1,2,0:T(8,128)(2,1)} async-done(((bf16[2,960,1280]{1,2,0:T(8,128)(2,1)}), bf16[1,960,1280]{1,2,0:T(8,128)(2,1)}) %reduce-scatter.15.cloned.1.call-update) | async-done | bytes 2457616 | tf_op jit(solution)/shard_map/reduce_scatter | solution.py:153
  398.2 4.3 copy.49
  402.6 4.1 reshape.241
  406.7 0.6 copy-done.20
  407.3 0.6 dynamic-slice
  407.9 51.6 %all-reduce.3.cloned.1.call-done = bf16[4,4,60,640]{3,1,2,0:T(4,128)(2,1)} async-done(((bf16[4,4,60,640]{3,1,2,0:T(4,128)(2,1)}), bf16[4,4,60,640]{3,1,2,0:T(4,128)(2,1)}) %all-reduce.3.cloned.1.call-update) | async-done | bytes 1228816
  459.5 1.7 dynamic-slice_bitcast_fusion
  461.2 0.8 copy.52
  462.0 3.6 all-to-all-start.1
  465.6 18.7 %reduce-scatter.23.cloned.1.call-done = bf16[1,160,480]{2,1,0:T(8,128)(2,1)} async-done(((bf16[4,160,480]{2,1,0:T(8,128)(2,1)}), bf16[1,160,480]{2,1,0:T(8,128)(2,1)}) %reduce-scatter.23.cloned.1.call-update) | async-done | bytes 153616 | tf_op jit(solution)/shard_map/reduce_scatter | solution.py:196
  484.3 1.7 bitcast_convert_fusion
  486.6 0.9 copy.57
  487.5 0.6 copy-done.19
  488.3 2.0 fusion.17
  490.4 39.4 %psum.7 = f32[2,960]{1,0:T(2,128)S(1)} all-reduce(f32[2,960]{1,0:T(2,128)S(1)} %pad_maximum_fusion.11), channel_id=1, replica_groups=mesh['dp'=2,'fsdp'=4,'ctx'=4] {'dp','fsdp','ctx'}, use_global_device_ids=true, to_apply=%region_9.10 | all-reduce | flops 1920 | bytes 15360 | tf_op jit(solution)/shard_map/psum | solution.py:249
  530.4 2.5 fusion.25
  532.9 39.0 %reduce-scatter.17.cloned.1.call-done = bf16[1,60,1280]{2,1,0:T(8,128)(2,1)} async-done(((bf16[16,60,1280]{2,1,0:T(8,128)(2,1)}), bf16[1,60,1280]{2,1,0:T(8,128)(2,1)}) %reduce-scatter.17.cloned.1.call-update) | async-done | bytes 153616 | tf_op jit(solution)/shard_map/reduce_scatter | solution.py:245
  571.9 1.6 slice_convert_fusion.1
  573.5 1.6 slice_convert_fusion.2
  (90 shorter events, 4.3 us)
Async XLA Ops:
  7.2 214.7 %copy-start = (bf16[640,960]{0,1:T(8,128)(2,1)S(1)}, bf16[640,960]{0,1:T(8,128)(2,1)}, u32[]{:S(2)}) copy-start(bf16[640,960]{0,1:T(8,128)(2,1)} %param.16) | copy-start | bytes 3686404
  7.2 49.8 %all-gather.8.cloned.1.call-start = ((), (), s32[]{:S(2)}) async-start(), calls=%async_computation.10 | async-start | bytes 3993600 | tf_op jit(solution)/shard_map/all_gather | solution.py:164
  7.9 87.6 %all-gather.14.cloned.1.call-start = ((), (), s32[]{:S(2)}) async-start(), calls=%async_computation.21 | async-start | bytes 1638400 | tf_op jit(solution)/shard_map/all_gather | solution.py:175
  61.0 0.8 copy-start.5
  62.6 68.0 %all-gather.10.cloned.1.call-start = ((), (), s32[]{:S(2)}) async-start(), calls=%async_computation.11 | async-start | bytes 2457600 | tf_op jit(solution)/shard_map/all_gather | solution.py:165
  63.4 132.0 %all-gather.12.cloned.1.call-start = ((), (), s32[]{:S(2)}) async-start(), calls=%async_computation.12 | async-start | bytes 2457600 | tf_op jit(solution)/shard_map/all_gather | solution.py:180
  95.5 1.3 copy-start.2
  130.6 2.6 copy-start.17
  133.2 135.7 %copy-start.4 = (f32[256,960]{0,1:T(8,128)}, f32[256,960]{0,1:T(8,128)S(1)}, u32[]{:S(2)}) copy-start(f32[256,960]{0,1:T(8,128)S(1)} %get-tuple-element.39) | copy-start | bytes 2949124
  134.3 87.6 %all-gather.16.cloned.1.call-start = ((), (), s32[]{:S(2)}) async-start(), calls=%async_computation.22 | async-start | bytes 2457600 | tf_op jit(solution)/shard_map/all_gather | solution.py:166
  134.9 134.0 %reduce-scatter.11.cloned.1.call-start = ((), (), s32[]{:S(2)}) async-start(), calls=%async_computation.14 | async-start | bytes 2457600 | tf_op jit(solution)/shard_map/reduce_scatter | solution.py:189
  221.9 8.7 %copy-start.6 = (bf16[4,240,1280]{2,1,0:T(8,128)(2,1)S(1)}, bf16[4,240,1280]{2,1,0:T(8,128)(2,1)}, u32[]{:S(2)}) copy-start(bf16[4,240,1280]{2,1,0:T(8,128)(2,1)} %all_to_all.10) | copy-start | bytes 7372804
  229.0 1.1 copy-start.21
  229.0 1.6 copy-start.22
  234.6 71.5 %reduce-scatter.9.cloned.1.call-start = ((), (), s32[]{:S(2)}) async-start(), calls=%async_computation.13 | async-start | bytes 2457600 | tf_op jit(solution)/shard_map/reduce_scatter | solution.py:191
  239.0 67.1 %copy-start.8 = (bf16[1,256,960]{1,2,0:T(8,128)(2,1)S(1)}, bf16[1,256,960]{1,2,0:T(8,128)(2,1)}, u32[]{:S(2)}) copy-start(bf16[1,256,960]{1,2,0:T(8,128)(2,1)} %param.17) | copy-start | bytes 1474564
  239.0 119.2 %reduce-scatter.13.cloned.1.call-start = ((), (), s32[]{:S(2)}) async-start(), calls=%async_computation.15 | async-start | bytes 1638400 | tf_op jit(solution)/shard_map/reduce_scatter | solution.py:227
  306.0 2.9 copy-start.7
  309.0 1.3 copy-start.3
  326.8 46.8 %reduce-scatter.19.cloned.1.call-start = ((), (), s32[]{:S(2)}) async-start(), calls=%async_computation.18 | async-start | bytes 3686400 | tf_op jit(solution)/shard_map/reduce_scatter | solution.py:153
  333.8 47.6 %reduce-scatter.21.cloned.1.call-start = ((), (), s32[]{:S(2)}) async-start(), calls=%async_computation.19 | async-start | bytes 1843200 | tf_op jit(solution)/shard_map/reduce_scatter | solution.py:153
  338.5 59.7 %reduce-scatter.15.cloned.1.call-start = ((), (), s32[]{:S(2)}) async-start(), calls=%async_computation.16 | async-start | bytes 7864320 | tf_op jit(solution)/shard_map/reduce_scatter | solution.py:153
  338.8 20.6 %copy-start.11 = (bf16[15,2,32,256]{3,2,1,0:T(8,128)(2,1)}, bf16[15,2,32,256]{3,2,1,0:T(8,128)(2,1)S(1)}, u32[]{:S(2)}) copy-start(bf16[15,2,32,256]{3,2,1,0:T(8,128)(2,1)S(1)} %pad_maximum_fusion.5) | copy-start | bytes 1474564
  338.8 20.6 %copy-start.9 = (bf16[1,256,960]{1,2,0:T(8,128)(2,1)S(1)}, bf16[1,256,960]{1,2,0:T(8,128)(2,1)}, u32[]{:S(2)}) copy-start(bf16[1,256,960]{1,2,0:T(8,128)(2,1)} %param.9) | copy-start | bytes 1474564
  338.8 20.6 %copy-start.18 = (f32[960]{0:T(1024)S(1)}, f32[960]{0:T(1024)}, u32[]{:S(2)}) copy-start(f32[960]{0:T(1024)} %param.11) | copy-start | bytes 11524
  359.2 2.9 copy-start.13
  359.4 2.8 copy-start.15
  373.6 85.9 %all-reduce.3.cloned.1.call-start = ((), (), s32[]{:S(2)}) async-start(), calls=%async_computation.23 | async-start | bytes 2457600
  377.1 107.2 %reduce-scatter.23.cloned.1.call-start = ((), (), s32[]{:S(2)}) async-start(), calls=%async_computation.20 | async-start | bytes 819200 | tf_op jit(solution)/shard_map/reduce_scatter | solution.py:196
  383.6 188.4 %reduce-scatter.17.cloned.1.call-start = ((), (), s32[]{:S(2)}) async-start(), calls=%async_computation.17 | async-start | bytes 2785280 | tf_op jit(solution)/shard_map/reduce_scatter | solution.py:245
  406.7 0.7 copy-start.20
  462.0 24.0 %all-to-all-start.1 = ((bf16[4,60,640]{2,1,0:T(8,128)(2,1)}), bf16[4,60,640]{2,1,0:T(8,128)(2,1)S(1)}, u32[]{:S(2)}, u32[]{:S(2)}) async-start(bf16[4,60,640]{2,1,0:T(8,128)(2,1)} %copy.52), calls=%async_computation.7 | async-start | bytes 655360 | tf_op jit(solution)/shard_map/all_to_all | solution.py:212
  486.0 2.1 copy-start.19
  486.0 2.2 copy-start.12
  486.0 2.2 copy-start.14
  486.1 2.2 copy-start.16
  488.3 42.1 %copy-start.10 = (bf16[1,256,960]{1,2,0:T(8,128)(2,1)S(1)}, bf16[1,256,960]{1,2,0:T(8,128)(2,1)}, u32[]{:S(2)}) copy-start(bf16[1,256,960]{1,2,0:T(8,128)(2,1)} %param.9) | copy-start | bytes 1474564
  530.4 44.7 %copy-start.1 = (bf16[640,960]{0,1:T(8,128)(2,1)S(1)}, bf16[640,960]{0,1:T(8,128)(2,1)}, u32[]{:S(2)}) copy-start(bf16[640,960]{0,1:T(8,128)(2,1)} %param.16) | copy-start | bytes 3686404
Sparse Core Ops, SparseCore 0:
  9.9 47.0 all-gather.7
  62.8 32.6 all-gather.13
  97.4 33.2 all-gather.9
  134.4 51.2 all-gather.11
  187.4 34.4 all-gather.15
  234.7 34.0 reduce-scatter.10
  271.9 34.0 reduce-scatter.8
  327.0 31.2 reduce-scatter.12
  360.5 8.7 reduce-scatter.18
  371.4 9.9 reduce-scatter.20
  383.8 14.3 reduce-scatter.14
  400.5 58.9 all-reduce.2
  462.5 21.8 reduce-scatter.22
  486.5 85.3 reduce-scatter.16

commit v2 on v1

v2 whole, which is shorter than its diff:
```python
import functools

import jax
import jax.numpy as jnp
from jax import lax
from jax.experimental import pallas as pl
from jax.experimental.pallas import tpu as pltpu
from jax.sharding import PartitionSpec as P

D = 960
HEADS = 15
KV_HEADS = 5
HD = 64
FF = 2560
GROUP = HEADS // KV_HEADS
KVW = KV_HEADS * HD
EPSILON = 1e-05
F32 = jnp.float32
BF16 = jnp.bfloat16


def dot(a, b, ca, cb):
    return lax.dot_general(a, b, (((ca,), (cb,)), ((), ())), preferred_element_type=F32)


def normalize(values, gain):
    return values * lax.rsqrt(jnp.mean(values * values, axis=-1, keepdims=True) + EPSILON) * gain


def angles_of(places):
    half = HD // 2
    frequency = 10000.0 ** (-jnp.arange(half, dtype=F32) / half)
    angles = frequency[:, None] * places.astype(F32)[None, :]
    return jnp.cos(angles), jnp.sin(angles)


def rotate(values, cosine, sine):
    length = values.shape[1]
    parts = values.reshape(-1, 2, HD // 2, length)
    front, back = parts[:, 0], parts[:, 1]
    turned = jnp.stack([front * cosine - back * sine, back * cosine + front * sine], axis=1)
    return turned.reshape(-1, length)


def keys_first(kv, which):
    pieces = [kv[c, which] for c in range(kv.shape[0])]
    return (
        jnp.concatenate([piece.T for piece in pieces], axis=0),
        jnp.concatenate(pieces, axis=1),
    )


def allowed_of(keys, rows):
    start = lax.axis_index("ctx") * rows
    key_at = lax.broadcasted_iota(jnp.int32, (keys, rows), 0)
    row_at = lax.broadcasted_iota(jnp.int32, (keys, rows), 1)
    return key_at <= row_at + start


def backward_kernel(q_ref, kv_ref, g_ref, lse_ref, dq_ref, dkv_ref):
    rows = q_ref.shape[1]
    kv = kv_ref[...]
    parts = kv.shape[0]
    keys, keys_t = keys_first(kv, 0)
    values, _ = keys_first(kv, 1)
    allowed = allowed_of(keys.shape[0], rows)
    dk = jnp.zeros((HD, keys.shape[0]), F32)
    dv = jnp.zeros((HD, keys.shape[0]), F32)
    for h in range(GROUP):
        q = q_ref[h * HD : (h + 1) * HD, :]
        g = g_ref[h * HD : (h + 1) * HD, :]
        scores = jnp.where(allowed, dot(keys, q, 1, 0), -1e30)
        prob = jnp.exp(scores - lse_ref[0, h : h + 1, :])
        dprob = dot(values, g, 1, 0)
        inner = jnp.sum(dprob * prob, axis=0, keepdims=True)
        ds = (prob * (dprob - inner)).astype(BF16)
        dq_ref[h * HD : (h + 1) * HD, :] = dot(keys_t, ds, 1, 0) * (HD**-0.5)
        dk = dk + dot(q, ds, 1, 1)
        dv = dv + dot(g, prob.astype(BF16), 1, 1)
    for c in range(parts):
        dkv_ref[c, 0] = dk[:, c * rows : (c + 1) * rows].astype(BF16)
        dkv_ref[c, 1] = dv[:, c * rows : (c + 1) * rows].astype(BF16)


def attention_specs(parts, rows):
    q_spec = pl.BlockSpec((GROUP * HD, rows), lambda g: (g, 0))
    kv_spec = pl.BlockSpec((parts, 2, HD, rows), lambda g: (0, 0, g, 0))
    lse_spec = pl.BlockSpec((1, GROUP, rows), lambda g: (g, 0, 0))
    return q_spec, kv_spec, lse_spec


def attention_backward(q, kv, g, lse):
    parts, rows = kv.shape[0], q.shape[1]
    q_spec, kv_spec, lse_spec = attention_specs(parts, rows)
    work = parts * rows * rows * HD * HEADS
    return pl.pallas_call(
        backward_kernel,
        grid=(KV_HEADS,),
        in_specs=[q_spec, kv_spec, q_spec, lse_spec],
        out_specs=[q_spec, kv_spec],
        out_shape=[
            jax.ShapeDtypeStruct((D, rows), F32),
            jax.ShapeDtypeStruct(kv.shape, BF16),
        ],
        compiler_params=pltpu.CompilerParams(vmem_limit_bytes=40 * 2**20),
        cost_estimate=pl.CostEstimate(
            flops=40 * work, bytes_accessed=5 * 2**20, transcendentals=work // HD
        ),
    )(q, kv, g, lse)


def halves(grad, dp):
    rows, columns = grad.shape
    return grad.reshape(rows, dp, columns // dp).transpose(1, 0, 2)


MESH = pl.DeviceIdType.MESH


def peer_of(axis, k):
    size = lax.axis_size(axis)
    return lax.rem(lax.axis_index(axis) + k, size)


def greet(axes):
    barrier = pltpu.get_barrier_semaphore()
    count = 0
    for axis in axes:
        for k in range(1, lax.axis_size(axis)):
            pl.semaphore_signal(
                barrier, inc=1, device_id={axis: peer_of(axis, k)}, device_id_type=MESH
            )
            count += 1
    pl.semaphore_wait(barrier, count)


def send(src, dst, sems, at, axis, k):
    copy = pltpu.make_async_remote_copy(
        src_ref=src,
        dst_ref=dst,
        send_sem=sems[0].at[at],
        recv_sem=sems[1].at[at],
        device_id={axis: peer_of(axis, k)},
        device_id_type=MESH,
    )
    copy.start()
    return copy


def swap_kernel(plan, *refs):
    count = len(plan)
    ins, outs = refs[:count], refs[count : 2 * count]
    local_sem, send_sem, recv_sem = refs[2 * count :]
    greet(sorted({axis for axis, _ in plan}))
    copies, at = [], 0
    for i, (axis, gather) in enumerate(plan):
        me = lax.axis_index(axis)
        own = ins[i] if gather else ins[i].at[me]
        copy = pltpu.make_async_copy(own, outs[i].at[me], local_sem.at[i])
        copy.start()
        copies.append(copy)
        for k in range(1, lax.axis_size(axis)):
            src = ins[i] if gather else ins[i].at[peer_of(axis, k)]
            copies.append(send(src, outs[i].at[me], (send_sem, recv_sem), at, axis, k))
            at += 1
    for copy in copies:
        copy.wait()


def swap(collective_id, *items):
    plan = [(axis, gather) for _, axis, gather in items]
    shapes = [
        jax.ShapeDtypeStruct(((lax.axis_size(axis),) + x.shape) if gather else x.shape, x.dtype)
        for x, axis, gather in items
    ]
    total = sum(lax.axis_size(axis) - 1 for axis, _ in plan)
    size = sum(shape.size * shape.dtype.itemsize for shape in shapes)
    return pl.pallas_call(
        functools.partial(swap_kernel, plan),
        in_specs=[pl.BlockSpec(memory_space=pl.ANY)] * len(plan),
        out_specs=[pl.BlockSpec(memory_space=pl.ANY)] * len(plan),
        out_shape=shapes,
        scratch_shapes=[
            pltpu.SemaphoreType.DMA((len(plan),)),
            pltpu.SemaphoreType.DMA((total,)),
            pltpu.SemaphoreType.DMA((total,)),
        ],
        compiler_params=pltpu.CompilerParams(collective_id=collective_id, has_side_effects=True),
        cost_estimate=pl.CostEstimate(flops=0, bytes_accessed=20 * size, transcendentals=0),
    )(*[x for x, _, _ in items])


def front_kernel(
    shared, qkv_in, out_in, gu_in, cot_in, normed, cosine, sine,
    qkv, out_all, gu_all, cot_all, q_ref, kv, att_ref, lse_ref,
    project, local_sem, send_sem, recv_sem, pass_send, pass_recv,
):
    fsdp, ctx = lax.axis_size("fsdp"), lax.axis_size("ctx")
    me, here = lax.axis_index("fsdp"), lax.axis_index("ctx")
    side = lax.axis_index("dp")
    rows = normed.shape[1]
    sems, pass_sems = (send_sem, recv_sem), (pass_send, pass_recv)
    greet(("fsdp", "ctx") + (("dp",) if shared else ()))
    locals_ = [
        pltpu.make_async_copy(qkv_in, qkv.at[me], local_sem.at[0]),
        pltpu.make_async_copy(out_in, out_all.at[me], local_sem.at[1]),
        pltpu.make_async_copy(gu_in.at[me], gu_all.at[me], local_sem.at[2]),
        pltpu.make_async_copy(cot_in, cot_all.at[me], local_sem.at[3]),
    ]
    for copy in locals_:
        copy.start()
    halves_of = lambda ref: ref.at[side] if shared else ref
    peers = range(1, fsdp)
    first = [
        send(halves_of(qkv_in), halves_of(qkv.at[me]), sems, k - 1, "fsdp", k) for k in peers
    ]
    rest, passed = [], []

    def hand_over(ref, base, arrivals):
        for k, copy in zip(peers, arrivals):
            copy.wait_recv()
            if shared:
                block = ref.at[lax.rem(me - k + fsdp, fsdp), side]
                passed.append(send(block, block, pass_sems, base + k - 1, "dp", 1))

    hand_over(qkv, 0, first)
    base = fsdp - 1
    seconds = [
        send(halves_of(out_in), halves_of(out_all.at[me]), sems, base + k - 1, "fsdp", k)
        for k in peers
    ]
    thirds = [
        send(
            halves_of(gu_in.at[peer_of("fsdp", k)]), halves_of(gu_all.at[me]), sems,
            2 * base + k - 1, "fsdp", k,
        )
        for k in peers
    ]
    lasts = [send(cot_in, cot_all.at[me], sems, 3 * base + k - 1, "fsdp", k) for k in peers]
    for copy in passed:
        copy.wait_recv()
    locals_[0].wait()
    blocks = 2 * fsdp
    total = jnp.zeros(project.shape[::-1], F32)
    for b in range(blocks):
        total = total + dot(normed[b], qkv[b // 2, b % 2], 1, 0)
    project[...] = total.T
    half = HD // 2
    cos, sin = cosine[...], sine[...]
    mine = kv.at[here]

    def turn(h, carry):
        start = pl.multiple_of(h * HD, HD)
        a = project[pl.ds(start, half), :]
        b = project[pl.ds(start + half, half), :]
        q_ref[pl.ds(start, HD), :] = (
            jnp.concatenate([a * cos - b * sin, b * cos + a * sin], axis=0) * (HD**-0.5)
        ).astype(BF16)
        return carry

    for h in range(KV_HEADS):
        at = D + h * HD
        a, b = project[at : at + half, :], project[at + half : at + HD, :]
        mine[0, h * HD : (h + 1) * HD, :] = jnp.concatenate(
            [a * cos - b * sin, b * cos + a * sin], axis=0
        ).astype(BF16)
    mine[1, :, :] = project[D + KVW :, :].astype(BF16)
    kvs = [
        send(mine, mine, sems, 4 * base + k - 1, "ctx", k) for k in range(1, ctx)
    ]
    lax.fori_loop(0, HEADS, turn, 0)
    hand_over(out_all, base, seconds)
    for copy in kvs:
        copy.wait()
    allowed = allowed_of(ctx * rows, rows)

    def attend(g, carry):
        at = pl.ds(pl.multiple_of(g * HD, HD), HD)
        keys = jnp.concatenate([kv[c, 0, at, :].T for c in range(ctx)], axis=0)
        values_t = jnp.concatenate([kv[c, 1, at, :] for c in range(ctx)], axis=1)
        for h in range(GROUP):
            spot = pl.ds(pl.multiple_of((g * GROUP + h) * HD, HD), HD)
            scores = jnp.where(allowed, dot(keys, q_ref[spot, :], 1, 0), -1e30)
            row_max = jnp.max(scores, axis=0, keepdims=True)
            exponent = jnp.exp(scores - row_max)
            sums = jnp.sum(exponent, axis=0, keepdims=True)
            att = dot(values_t, exponent.astype(BF16), 1, 0) / sums
            att_ref[spot, :] = att.astype(BF16)
            lse_ref[g, h : h + 1, :] = row_max + jnp.log(sums)
        return carry

    lax.fori_loop(0, KV_HEADS, attend, 0)
    hand_over(gu_all, 2 * base, thirds)
    for copy in lasts:
        copy.wait_recv()
    for copy in first + seconds + thirds + lasts:
        copy.wait_send()
    for i, copy in enumerate(passed):
        copy.wait_send()
        if i >= base:
            copy.wait_recv()
    for copy in locals_[1:]:
        copy.wait()


def front(qkv_in, out_in, gu_in, cot_in, normed, cosine, sine):
    fsdp, ctx, dp = lax.axis_size("fsdp"), lax.axis_size("ctx"), lax.axis_size("dp")
    rows = normed.shape[1]
    columns = qkv_in.shape[-1]
    sends = 4 * (fsdp - 1) + ctx - 1
    anywhere, vmem = pl.BlockSpec(memory_space=pl.ANY), pl.BlockSpec(memory_space=pltpu.VMEM)
    shape = jax.ShapeDtypeStruct
    return pl.pallas_call(
        functools.partial(front_kernel, dp == 2),
        in_specs=[anywhere] * 4 + [vmem] * 3,
        out_specs=[vmem, anywhere, anywhere, anywhere, vmem, vmem, vmem, vmem],
        out_shape=[
            shape((fsdp,) + qkv_in.shape, BF16),
            shape((fsdp,) + out_in.shape, BF16),
            shape(gu_in.shape, BF16),
            shape((fsdp,) + cot_in.shape, BF16),
            shape((D, rows), BF16),
            shape((ctx, 2, KVW, rows), BF16),
            shape((D, rows), BF16),
            shape((KV_HEADS, GROUP, rows), F32),
        ],
        scratch_shapes=[
            pltpu.VMEM((columns, rows), F32),
            pltpu.SemaphoreType.DMA((4,)),
            pltpu.SemaphoreType.DMA((sends,)),
            pltpu.SemaphoreType.DMA((sends,)),
            pltpu.SemaphoreType.DMA((3 * (fsdp - 1),)),
            pltpu.SemaphoreType.DMA((3 * (fsdp - 1),)),
        ],
        compiler_params=pltpu.CompilerParams(
            collective_id=0, has_side_effects=True, vmem_limit_bytes=48 * 2**20
        ),
        cost_estimate=pl.CostEstimate(
            flops=10**9, bytes_accessed=10**8, transcendentals=10**6
        ),
    )(qkv_in, out_in, gu_in, cot_in, normed, cosine, sine)


def padded(array, axis, to):
    widths = [(0, 0)] * array.ndim
    widths[axis] = (0, to - array.shape[axis])
    return jnp.pad(array, widths)


def shards(tokens, positions, gain_attn, gain_mlp, w_qkv, w_out, w_gu, w_down, cotangent):
    rows = tokens.shape[1]
    fsdp, ctx, dp = lax.axis_size("fsdp"), lax.axis_size("ctx"), lax.axis_size("dp")
    part = FF // fsdp
    own = D // fsdp
    slim = D // (fsdp * ctx)
    half, wide_half = own // 2, -(-own // 2 // 128) * 128
    pad = -(-slim // 16) * 16
    inputs = tokens[0].astype(F32)
    cosine, sine = angles_of(positions[0])
    gu_cut = w_gu.reshape(2, half, 2, fsdp, part).transpose(3, 0, 1, 2, 4)
    gu_cut = gu_cut.reshape(fsdp, 2, half, 2 * part)
    normed = normalize(inputs, gain_attn).astype(BF16)
    normed_cut = padded(normed.reshape(rows, 2 * fsdp, half).transpose(1, 0, 2), 2, wide_half)
    qkv_all, out_all, gu_all, cot_all, queries, every_kv, attended, lse = front(
        padded(w_qkv.reshape(2, half, -1), 1, wide_half),
        padded(w_out.reshape(2, half, D), 1, wide_half),
        padded(gu_cut, 2, wide_half),
        cotangent[0],
        normed_cut,
        cosine,
        sine,
    )
    full_qkv = qkv_all[:, :, :half].reshape(D, -1)
    full_out = out_all[:, :, :half].reshape(D, D)
    gu_part = gu_all[:, :, :half].reshape(D, 2 * part)
    cot_all = cot_all.reshape(fsdp * rows, D)

    hidden = inputs + dot(attended, full_out, 0, 0)
    normed_two = normalize(hidden, gain_mlp).astype(BF16)
    (two_all,) = swap(1, (normed_two, "fsdp", True))
    two_all = two_all.reshape(fsdp * rows, D)
    gate_up = dot(two_all, gu_part, 1, 0)
    gate, up = gate_up[:, :part], gate_up[:, part:]
    activated, swish_back = jax.vjp(lambda a, b: jax.nn.silu(a) * b, gate, up)
    activated = activated.astype(BF16)
    grad_activated = dot(cot_all, w_down, 1, 1)
    grad_gate, grad_up = swish_back(grad_activated)
    grad_gate_up = jnp.concatenate([grad_gate, grad_up], axis=1).astype(BF16)
    two_part = dot(grad_gate_up, gu_part, 1, 1).astype(BF16).reshape(fsdp, rows, D)
    down_part = dot(activated, w_down, 1, 0).astype(BF16).reshape(fsdp, rows, D)
    grad_down = halves(dot(activated, cot_all, 0, 0).astype(BF16), dp)

    def spread(array):
        array = array.reshape(-1, fsdp * ctx, slim)
        return padded(array, 2, pad).reshape(-1, fsdp * ctx * pad)

    grad_gu = dot(spread(two_all), grad_gate_up, 0, 0).astype(BF16)
    if dp == 2:
        grad_gu = halves(grad_gu, dp)
        two_sum, gu_sum, down_grads = swap(
            2, (two_part, "fsdp", False), (grad_gu, "dp", False), (grad_down, "dp", False)
        )
        gu_cols = total_of(gu_sum).astype(BF16)
    else:
        two_sum, down_grads = swap(2, (two_part, "fsdp", False), (grad_down, "dp", False))
        gu_cols = grad_gu
    grad_two = total_of(two_sum)
    down_grads = total_of(down_grads).astype(BF16).reshape(ctx, part // ctx, D // dp)
    gu_cols = gu_cols.reshape(fsdp, ctx, pad, -1).transpose(1, 0, 2, 3)

    grad_rows = cotangent[0].astype(F32)
    _, norm_back_two = jax.vjp(normalize, hidden, gain_mlp)
    grad_hidden_part, grad_gain_mlp = norm_back_two(grad_two)
    grad_hidden = grad_rows + grad_hidden_part
    grad_attn = grad_hidden.astype(BF16)
    grad_attended = dot(full_out, grad_attn, 1, 1).astype(BF16)
    attended_wide = padded(attended.reshape(fsdp * ctx, slim, rows), 1, pad).reshape(-1, rows)
    grad_out = dot(attended_wide, grad_attn, 1, 0).astype(BF16)
    grad_queries, kv_grads = attention_backward(queries, every_kv, grad_attended, lse)
    kv_sum, down_sum, result_down = swap(
        3,
        (kv_grads.reshape(ctx, 2 * KVW, rows), "ctx", False),
        (down_part, "fsdp", False),
        (down_grads, "ctx", False),
    )
    own_kv = total_of(kv_sum)
    outputs = hidden + total_of(down_sum)
    grad_project = jnp.concatenate(
        [
            rotate(grad_queries, cosine, -sine),
            rotate(own_kv[:KVW], cosine, -sine),
            own_kv[KVW:],
        ],
        axis=0,
    ).astype(BF16)
    grad_normed = dot(grad_project, full_qkv, 0, 1)
    grad_qkv = dot(spread(normed), grad_project, 0, 1).astype(BF16)
    _, norm_back_one = jax.vjp(normalize, inputs, gain_attn)
    grad_input_part, grad_gain_attn = norm_back_one(grad_normed)
    grad_inputs = grad_hidden + grad_input_part

    gains = jnp.stack([grad_gain_attn, grad_gain_mlp]).reshape(2, fsdp, ctx, slim)
    gains = padded(padded(gains.transpose(1, 2, 0, 3), 2, 8), 3, 128)
    both = jnp.concatenate([halves(grad_qkv, dp), halves(grad_out, dp)], axis=2)
    both, gains = swap(4, (both, "dp", False), (gains, "dp", True))
    both = total_of(both).astype(BF16).reshape(fsdp, ctx * pad, -1)
    both, gains, gu_sum = swap(
        5, (both, "fsdp", False), (total_of(gains), "fsdp", False), (gu_cols, "ctx", False)
    )
    both = total_of(both).astype(BF16).reshape(ctx, pad, -1)
    both, gains, gu_rows = swap(
        6,
        (both, "ctx", False),
        (total_of(gains), "ctx", False),
        (total_of(gu_sum).astype(BF16), "fsdp", False),
    )
    both, gains = total_of(both)[:slim], total_of(gains)[:2, :slim]
    gu_rows = gu_rows[:, :slim]
    if dp == 2:
        result_gu = gu_rows.transpose(1, 0, 2).reshape(slim, FF)
    else:
        gu_rows = gu_rows.reshape(fsdp, slim, 2, part).transpose(1, 2, 0, 3).reshape(slim, 2 * FF)
        result_gu = lax.psum_scatter(gu_rows, "dp", scatter_dimension=1, tiled=True)
    wide = w_qkv.shape[1] // dp
    return (
        outputs[None],
        grad_inputs[None],
        gains[0],
        gains[1],
        both[:, :wide],
        both[:, wide:],
        result_gu.astype(F32),
        total_of(result_down),
    )


def total_of(array):
    return jnp.sum(array.astype(F32), axis=0)


def solution(mesh):
    placed = (
        P(("dp", "fsdp"), "ctx", None),
        P(("dp", "fsdp"), "ctx"),
        P(),
        P(),
        P("fsdp", None),
        P("fsdp", None),
        P("fsdp", None),
        P("fsdp", None),
        P(("dp", "fsdp"), "ctx", None),
    )
    return jax.shard_map(
        shards,
        mesh=mesh,
        in_specs=placed,
        out_specs=(
            P(("dp", "fsdp"), "ctx", None),
            P(("dp", "fsdp"), "ctx", None),
            P(("fsdp", "ctx")),
            P(("fsdp", "ctx")),
            P(("fsdp", "ctx"), "dp"),
            P(("fsdp", "ctx"), "dp"),
            P(("fsdp", "ctx"), "dp"),
            P(("fsdp", "ctx"), "dp"),
        ),
        check_vma=False,
    )
```

time: 583 us -> 553 us (0.949); the launches traced: 582 us -> 545 us
  Pallas kernels: 27.6 us -> 377 us
  waiting for transfers between devices: 332 us -> 0 us
  blocking collectives: 82.5 us -> 0 us
  local copies, waits for them, and re-layouts: 50.6 us -> 88.5 us
  other arithmetic: 23.4 us -> 40.6 us
  between operations: 14.3 us -> 1.7 us
  matrix products: 46.5 us -> 36.6 us
    pallas_call x1 -> x7, Pallas kernels: 11.1 us -> 361 us  [the longest x6 284 us: swap(): pl.pallas_call(functools.partial(swap_kernel, plan), in_specs=[pl.BlockSp...]
    reduce_scatter x8 -> x0, waiting for transfers between devices: 159 us -> none  [the longest x1 39 us: shards(): lax.psum_scatter(both.reshape(fsdp * ctx, slim, -1), ('fsdp', 'ctx'), sca...]
    all_gather x5 -> x0, waiting for transfers between devices: 119 us -> none  [the longest x1 46.9 us: shards(): full_qkv = lax.all_gather(w_qkv, 'fsdp', axis=0, tiled=True)]
    unnamed x15 -> x0, waiting for transfers between devices: 53.6 us -> none
    all_to_all x1 -> x0, blocking collectives: 43 us -> none  [shards(): gu_part = lax.all_to_all(gu_cut, 'fsdp', 0, 0).reshape(D, 2 * part)]
    psum x1 -> x0, blocking collectives: 39.4 us -> none  [shards(): lax.psum(jnp.stack([grad_gain_attn, grad_gain_mlp]), ('dp', 'fsdp', 'ctx'))]
    reduce_sum x0 -> x13, other arithmetic: none -> 24.3 us  [total_of(): return jnp.sum(array.astype(F32), axis=0)]
    reshape x1 -> x4, local copies, waits for them, and re-layouts: 1.69 us -> 16.9 us  [halves(): return grad.reshape(rows, dp, columns // dp).transpose(1, 0, 2)]
  transfers between devices with their start and end apart: 15 -> 0, of which waited for: 12 -> 0; matrix products, arithmetic and copies ran while one was open for 15% -> 0% of each run, Pallas kernels for 2% -> 0%
where the time goes in v2:
time: 553 us; the launch traced here: 545 us
  Pallas kernels  377 us (68%)
  local copies, waits for them, and re-layouts  88.5 us (16%)
  other arithmetic  40.6 us (7%)
  matrix products  36.6 us (7%)
    pallas_call x6, Pallas kernels, swap(): pl.pallas_call(functools.partial(swap_kernel, plan), in_specs=[pl.BlockSp...  284 us
    pallas_call x1, Pallas kernels, front(): pl.pallas_call(functools.partial(front_kernel, dp == 2), in_specs=[anywhe...  76.9 us
    dot_general x11, matrix products, dot(): lax.dot_general(a, b, (((ca,), (cb,)), ((), ())), preferred_element_type=...  36.6 us
    reduce_sum x13, other arithmetic, total_of(): return jnp.sum(array.astype(F32), axis=0)  24.3 us
    reshape x4, local copies, waits for them, and re-layouts, halves(): return grad.reshape(rows, dp, columns // dp).transpose(1, 0, 2)  16.9 us
    pallas_call x1, Pallas kernels, attention_backward(): pl.pallas_call(backward_kernel, grid=(KV_HEADS,), in_specs=[q_spec, kv_sp...  15.8 us
    unnamed x79, local copies, waits for them, and re-layouts  12.9 us

profile of v2, /device:TPU:0, one launch (start us, length us, event | category | flops | bytes accessed | tf_op | source)
XLA Modules:
  0.0 544.6 jit_solution(12276202159979719745)
XLA Ops:
  0.7 1.4 copy.53
  2.2 1.1 convert_element_type.144
  3.3 1.5 copy.56
  6.2 5.6 %reshape.247 = bf16[2,120,2,4,640]{4,3,2,1,0:T(4,128)(2,1)} reshape(bf16[240,5120]{1,0:T(8,128)(2,1)} %param.15) | data formatting | bytes 4915200 | tf_op jit(solution)/shard_map/reshape | solution.py:360
  11.8 5.0 copy.80
  16.8 6.6 %reshape.248 = bf16[4,2,120,1280]{3,2,1,0:T(8,128)(2,1)} reshape(bf16[4,2,120,2,640]{4,3,2,1,0:T(2,128)(2,1)} %bitcast.102) | data formatting | bytes 4915200 | tf_op jit(solution)/shard_map/reshape | solution.py:361
  23.4 3.5 pad.38.gu_in
  27.0 76.9 %shard_map.152 = (bf16[4,2,128,1600]{3,2,1,0:T(8,128)(2,1)}, bf16[4,2,128,960]{3,2,1,0:T(8,128)(2,1)}, bf16[4,2,128,1280]{3,2,1,0:T(8,128)(2,1)}, bf16[4,256,960...) custom-call(bf16[2,128,1600]{2,1,0:T(8,128)(2,1)S(1)} %pad.36.qkv_in, ...), custom_call_target="tpu_custom_call" | custom-call | flops 1000000000 | bytes 100000000 | tf_op jit(solution)/shard_map/pallas_call | solution.py:313
  104.0 2.2 slice.55
  106.3 0.8 multiply_reduce_fusion.2
  107.5 1.0 copy-done.4
  108.5 0.9 multiply_convert_fusion.3.refs_0_
  109.4 25.3 %shard_map.153 = bf16[4,256,960]{2,1,0:T(8,128)(2,1)} custom-call(bf16[256,960]{1,0:T(8,128)(2,1)} %multiply_convert_fusion.3.refs_0_), custom_call_target="tpu_custom_call" | custom-call | bytes 39321600 | tf_op jit(solution)/shard_map/pallas_call | solution.py:178
  134.7 2.0 slice.56
  137.1 2.9 fusion.22
  140.0 4.1 fusion.2
  144.1 4.2 copy.61
  148.3 4.5 reshape_reshape.3
  152.8 2.0 pad.40
  155.1 4.3 convolution_convert_fusion.1
  159.4 4.6 copy.62
  163.9 4.4 copy.63
  168.4 6.5 %convolution_convert_fusion.2 = bf16[1024,960]{0,1:T(8,128)(2,1)} fusion(bf16[960,1280]{1,0:T(8,128)(2,1)} %bitcast.118, bf16[1024,640]{0,1:T(8,128)(2,1)} %get-tuple-element.85, bf16[1024,640]{0,1:T(8,128)(2,1)} %get-tuple-element.84), kind=kOutput, calls=%fused_computation.16 | convolution fusion | flops 2522808320 | bytes 7045120 | tf_op jit(solution)/shard_map/dot_general | solution.py:23
  174.8 4.1 copy.60
  178.9 4.8 convolution_convert_fusion.5
  183.7 2.4 copy.64
  186.1 78.1 %shard_map.154 = (bf16[4,256,960]{2,1,0:T(8,128)(2,1)}, bf16[2,1024,640]{2,1,0:T(8,128)(2,1)}, bf16[2,640,480]{2,1,0:T(8,128)(2,1)}) custom-call(bf16[4,256,960]{2,1,0:T(8,128)(2,1)} %bitcast.103, bf16[2,1024,640]{2,1,0:T(8,128)(2,1)} %bitcast.99, bf16[2,640,480]{2,1,0:T(8,128)(2,1)} %bitcast.110), custom_call_target="tpu_custom_call" | custom-call | bytes 116326400 | tf_op jit(solution)/shard_map/pallas_call | solution.py:178
  264.3 2.2 convert_reduce_fusion.1
  267.2 1.2 copy-done.8
  268.4 0.7 convolution_convert_fusion.6.g_ref
  269.3 0.7 copy-done.3
  270.1 15.8 %shard_map.155 = (f32[960,256]{1,0:T(8,128)S(1)}, bf16[4,2,320,256]{3,2,1,0:T(8,128)(2,1)S(1)}) custom-call(bf16[960,256]{1,0:T(8,128)(2,1)S(1)} %get-tuple-element.34.q_ref, bf16[4,2,320,256]{3,2,1,0:T(8,128)(2,1)S(1)} %copy-done.3, bf16[960,256]{1,0:T(8,128)(2,1)S(1)} %convolution_convert_fusion.6.g_ref, f32[5,3,256]{2,1,0:T(4,128)S(1)} %get-tuple-element.39.lse_ref), custom_call_target="tpu_custom_call" | custom-call | flops 10066329600 | bytes 5242880 | tf_op jit(solution)/shard_map/pallas_call | solution.py:96
  285.9 1.1 copy-done.1
  287.1 0.8 pad_maximum_fusion.5
  288.5 1.3 reduce_sum.214
  289.8 4.3 convolution_convert_fusion.4
  294.1 3.9 copy.65
  298.0 43.8 %shard_map.156 = (bf16[4,640,256]{2,1,0:T(8,128)(2,1)}, bf16[4,256,960]{2,1,0:T(8,128)(2,1)}, bf16[4,160,480]{2,1,0:T(8,128)(2,1)}) custom-call(bf16[4,640,256]{2,1,0:T(8,128)(2,1)} %bitcast.93, bf16[4,256,960]{2,1,0:T(8,128)(2,1)} %bitcast.105, bf16[4,160,480]{2,1,0:T(8,128)(2,1)} %bitcast.114), custom_call_target="tpu_custom_call" | custom-call | bytes 77824000 | tf_op jit(solution)/shard_map/pallas_call | solution.py:178
  341.8 1.7 convert_reduce_fusion.2
  344.4 1.0 copy-done.11
  345.5 2.2 fusion.10
  348.5 1.1 reshape.275
  349.7 1.5 multiply_convert_fusion.2
  351.3 2.7 convolution_convert_fusion
  354.0 6.0 %copy.67 = bf16[1024,2,800]{2,0,1:T(8,128)(2,1)} copy(bf16[1024,2,800]{0,2,1:T(8,128)(2,1)} %bitcast.97) | data formatting | bytes 6553600 | tf_op jit(solution)/shard_map/reshape | solution.py:114
  360.2 3.2 convolution_convert_fusion.3
  363.4 4.1 copy.68
  367.5 6.4 %pad_maximum_fusion.refs_0_ = bf16[2,1024,1280]{2,1,0:T(8,128)(2,1)} fusion(bf16[2,1024,480]{2,1,0:T(8,128)(2,1)} %bitcast.106, bf16[2,1024,800]{2,1,0:T(8,128)(2,1)} %bitcast.98), kind=kLoop, calls=%fused_computation | loop fusion | flops 10485760 | bytes 10485760 | tf_op jit(solution)/shard_map/concatenate | solution.py:444
  374.0 82.6 %shard_map.157 = (bf16[2,1024,1280]{2,1,0:T(8,128)(2,1)}, f32[2,4,4,8,128]{4,3,2,1,0:T(8,128)}) custom-call(bf16[2,1024,1280]{2,1,0:T(8,128)(2,1)} %pad_maximum_fusion.refs_0_, f32[4,4,8,128]{3,2,1,0:T(8,128)} %pad.58.refs_1_), custom_call_target="tpu_custom_call" | custom-call | bytes 107479040 | tf_op jit(solution)/shard_map/pallas_call | solution.py:178
  456.6 5.7 %reduce_sum.220 = bf16[1024,1280]{1,0:T(8,128)(2,1)} reduce(bf16[2,1024,1280]{2,1,0:T(8,128)(2,1)} %get-tuple-element.46, bf16[]{:T(256)} %constant.21.clone.1), dimensions={0}, to_apply=%region_10.11 | reduce | flops 1310720 | bytes 7864322 | tf_op jit(solution)/shard_map/reduce_sum | solution.py:478
  462.9 3.7 reduce_sum.222
  466.6 2.5 copy.81
  469.1 36.4 %shard_map.158 = (bf16[4,256,1280]{2,1,0:T(8,128)(2,1)}, f32[4,4,8,128]{3,2,1,0:T(8,128)}, bf16[4,4,64,640]{3,2,1,0:T(8,128)(2,1)}) custom-call(bf16[4,256,1280]{2,1,0:T(8,128)(2,1)} %bitcast.100, f32[4,4,8,128]{3,2,1,0:T(8,128)} %reduce_sum.221.refs_1_, bf16[4,4,64,640]{3,2,1,0:T(8,128)(2,1)} %bitcast.108), custom_call_target="tpu_custom_call" | custom-call | bytes 79953920 | tf_op jit(solution)/shard_map/pallas_call | solution.py:178
  505.6 3.1 reduce_sum.223
  508.7 2.3 reduce_sum.225.refs_2_
  511.7 18.1 %shard_map.159 = (bf16[4,64,1280]{2,1,0:T(8,128)(2,1)}, f32[4,8,128]{2,1,0:T(8,128)}, bf16[4,64,640]{2,1,0:T(8,128)(2,1)}) custom-call(bf16[4,64,1280]{2,1,0:T(8,128)(2,1)} %bitcast.116, f32[4,8,128]{2,1,0:T(8,128)} %reduce_sum.224.refs_1_, bf16[4,64,640]{2,1,0:T(8,128)(2,1)} %reduce_sum.225.refs_2_), custom_call_target="tpu_custom_call" | custom-call | bytes 19988480 | tf_op jit(solution)/shard_map/pallas_call | solution.py:178
  529.8 1.0 convert_bitcast_fusion
  531.4 0.9 copy.77
  533.1 0.8 slice.80
  534.4 2.8 fusion.6
  537.2 2.6 copy.73
  539.8 2.1 convert_reduce_fusion
  542.1 1.3 copy.72
  543.3 0.8 convert_reduce_fusion.3
  (108 shorter events, 9.6 us)
Async XLA Ops:
  0.6 139.4 %copy-start = (bf16[640,960]{0,1:T(8,128)(2,1)S(1)}, bf16[640,960]{0,1:T(8,128)(2,1)}, u32[]{:S(2)}) copy-start(bf16[640,960]{0,1:T(8,128)(2,1)} %param.16) | copy-start | bytes 3686404
  0.6 1.6 copy-start.14
  2.0 2.8 copy-start.9
  2.0 2.8 copy-start.30
  3.3 2.0 copy-start.33
  5.0 1.0 copy-start.27
  23.4 3.5 copy-start.21
  23.4 3.5 copy-start.26
  104.0 3.1 copy-start.2
  104.0 2.3 copy-start.10
  106.2 1.3 copy-start.7
  106.3 2.2 copy-start.31
  107.5 1.0 copy-start.4
  134.7 2.3 copy-start.13
  136.7 3.3 copy-start.17
  137.1 3.0 copy-start.34
  152.8 2.0 copy-start.35
  152.8 2.3 copy-start.36
  264.3 2.2 copy-start.5
  266.8 1.5 copy-start.8
  268.4 1.0 copy-start.12
  268.4 1.7 copy-start.3
  285.9 1.1 copy-start.1
  287.0 1.5 copy-start.20
  341.8 2.4 copy-start.16
  343.7 0.7 copy-start.22
  344.2 1.2 copy-start.11
  344.2 1.3 copy-start.18
  345.5 3.0 copy-start.15
  349.6 1.6 copy-start.19
  349.7 1.6 copy-start.23
  456.5 5.7 %copy-start.28 = (f32[2,4,4,8,128]{4,3,2,1,0:T(8,128)S(1)}, f32[2,4,4,8,128]{4,3,2,1,0:T(8,128)}, u32[]{:S(2)}) copy-start(f32[2,4,4,8,128]{4,3,2,1,0:T(8,128)} %get-tuple-element.47) | copy-start | bytes 393220
  505.6 5.5 %copy-start.29 = (f32[4,4,8,128]{3,2,1,0:T(8,128)S(1)}, f32[4,4,8,128]{3,2,1,0:T(8,128)}, u32[]{:S(2)}) copy-start(f32[4,4,8,128]{3,2,1,0:T(8,128)} %get-tuple-element.50) | copy-start | bytes 196612
  530.8 1.4 copy-start.25
  531.3 2.6 copy-start.32
  537.2 4.7 copy-start.6
  542.1 1.3 copy-start.24

commit v3 on v2

--- a/solution.py
+++ b/solution.py
@@ -109,11 +109,6 @@
     )(q, kv, g, lse)
 
 
-def halves(grad, dp):
-    rows, columns = grad.shape
-    return grad.reshape(rows, dp, columns // dp).transpose(1, 0, 2)
-
-
 MESH = pl.DeviceIdType.MESH
 
 
@@ -150,17 +145,20 @@
 def swap_kernel(plan, *refs):
     count = len(plan)
     ins, outs = refs[:count], refs[count : 2 * count]
-    local_sem, send_sem, recv_sem = refs[2 * count :]
+    send_sem, recv_sem = refs[2 * count :]
     greet(sorted({axis for axis, _ in plan}))
     copies, at = [], 0
-    for i, (axis, gather) in enumerate(plan):
+    for i, (axis, kind) in enumerate(plan):
         me = lax.axis_index(axis)
-        own = ins[i] if gather else ins[i].at[me]
-        copy = pltpu.make_async_copy(own, outs[i].at[me], local_sem.at[i])
-        copy.start()
-        copies.append(copy)
         for k in range(1, lax.axis_size(axis)):
-            src = ins[i] if gather else ins[i].at[peer_of(axis, k)]
+            there = peer_of(axis, k)
+            if kind == "all":
+                src = ins[i]
+            elif kind == "rows":
+                src = ins[i].at[there]
+            else:
+                width = outs[i].shape[-1]
+                src = ins[i].at[:, pl.ds(pl.multiple_of(there * width, 128), width)]
             copies.append(send(src, outs[i].at[me], (send_sem, recv_sem), at, axis, k))
             at += 1
     for copy in copies:
@@ -168,11 +166,17 @@
 
 
 def swap(collective_id, *items):
-    plan = [(axis, gather) for _, axis, gather in items]
-    shapes = [
-        jax.ShapeDtypeStruct(((lax.axis_size(axis),) + x.shape) if gather else x.shape, x.dtype)
-        for x, axis, gather in items
-    ]
+    plan = [(axis, kind) for _, axis, kind in items]
+
+    def shape_of(x, axis, kind):
+        size = lax.axis_size(axis)
+        if kind == "all":
+            return (size,) + x.shape
+        if kind == "rows":
+            return x.shape
+        return (size, x.shape[0], x.shape[1] // size)
+
+    shapes = [jax.ShapeDtypeStruct(shape_of(*item), item[0].dtype) for item in items]
     total = sum(lax.axis_size(axis) - 1 for axis, _ in plan)
     size = sum(shape.size * shape.dtype.itemsize for shape in shapes)
     return pl.pallas_call(
@@ -181,7 +185,6 @@
         out_specs=[pl.BlockSpec(memory_space=pl.ANY)] * len(plan),
         out_shape=shapes,
         scratch_shapes=[
-            pltpu.SemaphoreType.DMA((len(plan),)),
             pltpu.SemaphoreType.DMA((total,)),
             pltpu.SemaphoreType.DMA((total,)),
         ],
@@ -199,13 +202,31 @@
     me, here = lax.axis_index("fsdp"), lax.axis_index("ctx")
     side = lax.axis_index("dp")
     rows = normed.shape[1]
+    part = FF // fsdp
+
+    def columns_of(place, device):
+        return pl.ds(pl.multiple_of(place * FF + device * part, 128), part)
+
+    def gu_block(place, k):
+        columns = columns_of(place, peer_of("fsdp", k))
+        mine = pl.ds(place * part, part)
+        if shared:
+            return gu_in.at[side, :, columns], gu_all.at[me, side, :, mine]
+        return gu_in.at[:, :, columns], gu_all.at[me, :, :, mine]
+
     sems, pass_sems = (send_sem, recv_sem), (pass_send, pass_recv)
     greet(("fsdp", "ctx") + (("dp",) if shared else ()))
     locals_ = [
         pltpu.make_async_copy(qkv_in, qkv.at[me], local_sem.at[0]),
         pltpu.make_async_copy(out_in, out_all.at[me], local_sem.at[1]),
-        pltpu.make_async_copy(gu_in.at[me], gu_all.at[me], local_sem.at[2]),
-        pltpu.make_async_copy(cot_in, cot_all.at[me], local_sem.at[3]),
+        pltpu.make_async_copy(cot_in, cot_all.at[me], local_sem.at[2]),
+    ] + [
+        pltpu.make_async_copy(
+            gu_in.at[:, :, columns_of(place, me)],
+            gu_all.at[me, :, :, place * part : (place + 1) * part],
+            local_sem.at[3 + place],
+        )
+        for place in range(2)
     ]
     for copy in locals_:
         copy.start()
@@ -230,13 +251,12 @@
         for k in peers
     ]
     thirds = [
-        send(
-            halves_of(gu_in.at[peer_of("fsdp", k)]), halves_of(gu_all.at[me]), sems,
-            2 * base + k - 1, "fsdp", k,
-        )
-        for k in peers
-    ]
-    lasts = [send(cot_in, cot_all.at[me], sems, 3 * base + k - 1, "fsdp", k) for k in peers]
+        send(*gu_block(0, k), sems, 2 * base + k - 1, "fsdp", k) for k in peers
+    ]
+    fourths = [
+        send(*gu_block(1, k), sems, 3 * base + k - 1, "fsdp", k) for k in peers
+    ]
+    lasts = [send(cot_in, cot_all.at[me], sems, 4 * base + k - 1, "fsdp", k) for k in peers]
     for copy in passed:
         copy.wait_recv()
     locals_[0].wait()
@@ -266,7 +286,7 @@
         ).astype(BF16)
     mine[1, :, :] = project[D + KVW :, :].astype(BF16)
     kvs = [
-        send(mine, mine, sems, 4 * base + k - 1, "ctx", k) for k in range(1, ctx)
+        send(mine, mine, sems, 5 * base + k - 1, "ctx", k) for k in range(1, ctx)
     ]
     lax.fori_loop(0, HEADS, turn, 0)
     hand_over(out_all, base, seconds)
@@ -290,10 +310,12 @@
         return carry
 
     lax.fori_loop(0, KV_HEADS, attend, 0)
+    for copy in fourths:
+        copy.wait_recv()
     hand_over(gu_all, 2 * base, thirds)
     for copy in lasts:
         copy.wait_recv()
-    for copy in first + seconds + thirds + lasts:
+    for copy in first + seconds + thirds + fourths + lasts:
         copy.wait_send()
     for i, copy in enumerate(passed):
         copy.wait_send()
@@ -307,17 +329,17 @@
     fsdp, ctx, dp = lax.axis_size("fsdp"), lax.axis_size("ctx"), lax.axis_size("dp")
     rows = normed.shape[1]
     columns = qkv_in.shape[-1]
-    sends = 4 * (fsdp - 1) + ctx - 1
+    sends = 5 * (fsdp - 1) + ctx - 1
     anywhere, vmem = pl.BlockSpec(memory_space=pl.ANY), pl.BlockSpec(memory_space=pltpu.VMEM)
     shape = jax.ShapeDtypeStruct
     return pl.pallas_call(
         functools.partial(front_kernel, dp == 2),
         in_specs=[anywhere] * 4 + [vmem] * 3,
-        out_specs=[vmem, anywhere, anywhere, anywhere, vmem, vmem, vmem, vmem],
+        out_specs=[vmem] * 8,
         out_shape=[
             shape((fsdp,) + qkv_in.shape, BF16),
             shape((fsdp,) + out_in.shape, BF16),
-            shape(gu_in.shape, BF16),
+            shape((fsdp,) + gu_in.shape[:2] + (2 * FF // fsdp,), BF16),
             shape((fsdp,) + cot_in.shape, BF16),
             shape((D, rows), BF16),
             shape((ctx, 2, KVW, rows), BF16),
@@ -326,7 +348,7 @@
         ],
         scratch_shapes=[
             pltpu.VMEM((columns, rows), F32),
-            pltpu.SemaphoreType.DMA((4,)),
+            pltpu.SemaphoreType.DMA((5,)),
             pltpu.SemaphoreType.DMA((sends,)),
             pltpu.SemaphoreType.DMA((sends,)),
             pltpu.SemaphoreType.DMA((3 * (fsdp - 1),)),
@@ -357,14 +379,12 @@
     pad = -(-slim // 16) * 16
     inputs = tokens[0].astype(F32)
     cosine, sine = angles_of(positions[0])
-    gu_cut = w_gu.reshape(2, half, 2, fsdp, part).transpose(3, 0, 1, 2, 4)
-    gu_cut = gu_cut.reshape(fsdp, 2, half, 2 * part)
     normed = normalize(inputs, gain_attn).astype(BF16)
     normed_cut = padded(normed.reshape(rows, 2 * fsdp, half).transpose(1, 0, 2), 2, wide_half)
     qkv_all, out_all, gu_all, cot_all, queries, every_kv, attended, lse = front(
         padded(w_qkv.reshape(2, half, -1), 1, wide_half),
         padded(w_out.reshape(2, half, D), 1, wide_half),
-        padded(gu_cut, 2, wide_half),
+        padded(w_gu.reshape(2, half, 2 * FF), 1, wide_half),
         cotangent[0],
         normed_cut,
         cosine,
@@ -377,8 +397,8 @@
 
     hidden = inputs + dot(attended, full_out, 0, 0)
     normed_two = normalize(hidden, gain_mlp).astype(BF16)
-    (two_all,) = swap(1, (normed_two, "fsdp", True))
-    two_all = two_all.reshape(fsdp * rows, D)
+    (two_all,) = swap(1, (normed_two, "fsdp", "all"))
+    two_all = with_own(two_all, normed_two, "fsdp").reshape(fsdp * rows, D)
     gate_up = dot(two_all, gu_part, 1, 0)
     gate, up = gate_up[:, :part], gate_up[:, part:]
     activated, swish_back = jax.vjp(lambda a, b: jax.nn.silu(a) * b, gate, up)
@@ -388,7 +408,7 @@
     grad_gate_up = jnp.concatenate([grad_gate, grad_up], axis=1).astype(BF16)
     two_part = dot(grad_gate_up, gu_part, 1, 1).astype(BF16).reshape(fsdp, rows, D)
     down_part = dot(activated, w_down, 1, 0).astype(BF16).reshape(fsdp, rows, D)
-    grad_down = halves(dot(activated, cot_all, 0, 0).astype(BF16), dp)
+    grad_down = dot(activated, in_halves(cot_all, 1, dp), 0, 0).astype(BF16)
 
     def spread(array):
         array = array.reshape(-1, fsdp * ctx, slim)
@@ -396,16 +416,19 @@
 
     grad_gu = dot(spread(two_all), grad_gate_up, 0, 0).astype(BF16)
     if dp == 2:
-        grad_gu = halves(grad_gu, dp)
-        two_sum, gu_sum, down_grads = swap(
-            2, (two_part, "fsdp", False), (grad_gu, "dp", False), (grad_down, "dp", False)
+        two_sum, down_grads, gu_sum = swap(
+            2,
+            (two_part, "fsdp", "rows"),
+            (grad_down, "dp", "columns"),
+            (grad_gu, "dp", "columns"),
         )
-        gu_cols = total_of(gu_sum).astype(BF16)
+        gu_cols = total_of(gu_sum, grad_gu, "dp", "columns").astype(BF16)
     else:
-        two_sum, down_grads = swap(2, (two_part, "fsdp", False), (grad_down, "dp", False))
+        two_sum, down_grads = swap(2, (two_part, "fsdp", "rows"), (grad_down, "dp", "columns"))
         gu_cols = grad_gu
-    grad_two = total_of(two_sum)
-    down_grads = total_of(down_grads).astype(BF16).reshape(ctx, part // ctx, D // dp)
+    grad_two = total_of(two_sum, two_part, "fsdp", "rows")
+    down_grads = total_of(down_grads, grad_down, "dp", "columns").astype(BF16)
+    down_grads = down_grads.reshape(ctx, part // ctx, -1)
     gu_cols = gu_cols.reshape(fsdp, ctx, pad, -1).transpose(1, 0, 2, 3)
 
     grad_rows = cotangent[0].astype(F32)
@@ -415,16 +438,15 @@
     grad_attn = grad_hidden.astype(BF16)
     grad_attended = dot(full_out, grad_attn, 1, 1).astype(BF16)
     attended_wide = padded(attended.reshape(fsdp * ctx, slim, rows), 1, pad).reshape(-1, rows)
-    grad_out = dot(attended_wide, grad_attn, 1, 0).astype(BF16)
+    grad_out = dot(attended_wide, in_halves(grad_attn, 1, dp), 1, 0).astype(BF16)
     grad_queries, kv_grads = attention_backward(queries, every_kv, grad_attended, lse)
-    kv_sum, down_sum, result_down = swap(
-        3,
-        (kv_grads.reshape(ctx, 2 * KVW, rows), "ctx", False),
-        (down_part, "fsdp", False),
-        (down_grads, "ctx", False),
-    )
-    own_kv = total_of(kv_sum)
-    outputs = hidden + total_of(down_sum)
+    kv_grads = kv_grads.reshape(ctx, 2 * KVW, rows)
+    kv_sum, down_sum, last_down = swap(
+        3, (kv_grads, "ctx", "rows"), (down_part, "fsdp", "rows"), (down_grads, "ctx", "rows")
+    )
+    own_kv = total_of(kv_sum, kv_grads, "ctx", "rows")
+    outputs = hidden + total_of(down_sum, down_part, "fsdp", "rows")
+    result_down = total_of(last_down, down_grads, "ctx", "rows")[:, : D // dp]
     grad_project = jnp.concatenate(
         [
             rotate(grad_queries, cosine, -sine),
@@ -434,48 +456,81 @@
         axis=0,
     ).astype(BF16)
     grad_normed = dot(grad_project, full_qkv, 0, 1)
-    grad_qkv = dot(spread(normed), grad_project, 0, 1).astype(BF16)
+    grad_qkv = dot(spread(normed), in_halves(grad_project, 0, dp), 0, 1).astype(BF16)
     _, norm_back_one = jax.vjp(normalize, inputs, gain_attn)
     grad_input_part, grad_gain_attn = norm_back_one(grad_normed)
     grad_inputs = grad_hidden + grad_input_part
 
     gains = jnp.stack([grad_gain_attn, grad_gain_mlp]).reshape(2, fsdp, ctx, slim)
     gains = padded(padded(gains.transpose(1, 2, 0, 3), 2, 8), 3, 128)
-    both = jnp.concatenate([halves(grad_qkv, dp), halves(grad_out, dp)], axis=2)
-    both, gains = swap(4, (both, "dp", False), (gains, "dp", True))
-    both = total_of(both).astype(BF16).reshape(fsdp, ctx * pad, -1)
-    both, gains, gu_sum = swap(
-        5, (both, "fsdp", False), (total_of(gains), "fsdp", False), (gu_cols, "ctx", False)
-    )
-    both = total_of(both).astype(BF16).reshape(ctx, pad, -1)
-    both, gains, gu_rows = swap(
-        6,
-        (both, "ctx", False),
-        (total_of(gains), "ctx", False),
-        (total_of(gu_sum).astype(BF16), "fsdp", False),
-    )
-    both, gains = total_of(both)[:slim], total_of(gains)[:2, :slim]
+    arrived = swap(4, (grad_qkv, "dp", "columns"), (grad_out, "dp", "columns"), (gains, "dp", "all"))
+    sent = [
+        total_of(arrived[0], grad_qkv, "dp", "columns").astype(BF16).reshape(fsdp, ctx * pad, -1),
+        total_of(arrived[1], grad_out, "dp", "columns").astype(BF16).reshape(fsdp, ctx * pad, -1),
+        total_of(arrived[2], gains, "dp", "all"),
+        gu_cols,
+    ]
+    arrived = swap(
+        5, *[(x, axis, "rows") for x, axis in zip(sent, ("fsdp", "fsdp", "fsdp", "ctx"))]
+    )
+    sent = [
+        total_of(arrived[0], sent[0], "fsdp", "rows").astype(BF16).reshape(ctx, pad, -1),
+        total_of(arrived[1], sent[1], "fsdp", "rows").astype(BF16).reshape(ctx, pad, -1),
+        total_of(arrived[2], sent[2], "fsdp", "rows"),
+        total_of(arrived[3], sent[3], "ctx", "rows").astype(BF16),
+    ]
+    arrived = swap(
+        6, *[(x, axis, "rows") for x, axis in zip(sent, ("ctx", "ctx", "ctx", "fsdp"))]
+    )
+    result_qkv, result_out, gains = [
+        total_of(arrived[i], sent[i], "ctx", "rows") for i in range(3)
+    ]
+    gains = gains[:2, :slim]
+    own_gu = lax.dynamic_index_in_dim(sent[3], lax.axis_index("fsdp"), 0, keepdims=False)
+    gu_rows = with_own(arrived[3], own_gu, "fsdp")
     gu_rows = gu_rows[:, :slim]
     if dp == 2:
         result_gu = gu_rows.transpose(1, 0, 2).reshape(slim, FF)
     else:
         gu_rows = gu_rows.reshape(fsdp, slim, 2, part).transpose(1, 2, 0, 3).reshape(slim, 2 * FF)
         result_gu = lax.psum_scatter(gu_rows, "dp", scatter_dimension=1, tiled=True)
-    wide = w_qkv.shape[1] // dp
     return (
         outputs[None],
         grad_inputs[None],
         gains[0],
         gains[1],
-        both[:, :wide],
-        both[:, wide:],
+        result_qkv[:slim, : w_qkv.shape[1] // dp],
+        result_out[:slim, : D // dp],
         result_gu.astype(F32),
-        total_of(result_down),
-    )
-
-
-def total_of(array):
-    return jnp.sum(array.astype(F32), axis=0)
+        result_down,
+    )
+
+
+def total_of(received, sent, axis, kind):
+    me, size = lax.axis_index(axis), lax.axis_size(axis)
+    if kind == "all":
+        own = sent
+    elif kind == "rows":
+        own = lax.dynamic_index_in_dim(sent, me, 0, keepdims=False)
+    else:
+        width = received.shape[-1]
+        own = lax.dynamic_slice_in_dim(sent, me * width, width, 1)
+    total = own.astype(F32)
+    for j in range(size):
+        total = total + jnp.where(me == j, 0.0, received[j].astype(F32))
+    return total
+
+
+def with_own(received, own, axis):
+    return lax.dynamic_update_index_in_dim(received, own, lax.axis_index(axis), 0)
+
+
+def in_halves(array, axis, count):
+    size = array.shape[axis] // count
+    to = -(-size // 128) * 128
+    shape = array.shape[:axis] + (count, size) + array.shape[axis + 1 :]
+    flat = array.shape[:axis] + (count * to,) + array.shape[axis + 1 :]
+    return padded(array.reshape(shape), axis + 1, to).reshape(flat)
 
 
 def solution(mesh):

time: 553 us -> 406 us (0.73); the launches traced: 545 us -> 404 us
  Pallas kernels: 377 us -> 253 us
  local copies, waits for them, and re-layouts: 88.5 us -> 69.4 us
  other arithmetic: 40.6 us -> 49.1 us
  matrix products: 36.6 us -> 30.6 us
    pallas_call x6, Pallas kernels: 284 us -> 158 us  [swap(): pl.pallas_call(functools.partial(swap_kernel, plan), in_specs=[pl.BlockSp...]
    reshape x7 -> x0, local copies, waits for them, and re-layouts: 34.1 us -> none  [the longest x4 16.9 us: halves(): return grad.reshape(rows, dp, columns // dp).transpose(1, 0, 2)]
    reduce_sum x13 -> x0, other arithmetic: 24.3 us -> none  [total_of(): return jnp.sum(array.astype(F32), axis=0)]
    convert_element_type x0 -> x9, other arithmetic: none -> 20.9 us  [the longest x1 4.73 us: shards(): total_of(arrived[0], grad_qkv, 'dp', 'columns').astype(BF16)]
    another operation x0 -> x2, local copies, waits for them, and re-layouts: none -> 10.9 us  [in_halves(): return padded(array.reshape(shape), axis + 1, to).reshape(flat)]
    add x1 -> x7, other arithmetic: 0.32 us -> 10.5 us  [total_of(): total = total + jnp.where(me == j, 0.0, received[j].astype(F32))]
    concatenate x1 -> x0, other arithmetic: 6.44 us -> none  [shards(): both = jnp.concatenate([halves(grad_qkv, dp), halves(grad_out, dp)], axis=2)]
    dot_general x11, matrix products: 36.6 us -> 30.6 us  [dot(): lax.dot_general(a, b, (((ca,), (cb,)), ((), ())), preferred_element_type=...]
where the time goes in v3:
time: 406 us; the launch traced here: 404 us
  Pallas kernels  253 us (62%)
  local copies, waits for them, and re-layouts  69.4 us (17%)
  other arithmetic  49.1 us (12%)
  matrix products  30.6 us (8%)
    pallas_call x6, Pallas kernels, swap(): pl.pallas_call(functools.partial(swap_kernel, plan), in_specs=[pl.BlockSp...  158 us
    pallas_call x1, Pallas kernels, front(): pl.pallas_call(functools.partial(front_kernel, dp == 2), in_specs=[anywhe...  79.1 us
    dot_general x11, matrix products, dot(): lax.dot_general(a, b, (((ca,), (cb,)), ((), ())), preferred_element_type=...  30.6 us
    pallas_call x1, Pallas kernels, attention_backward(): pl.pallas_call(backward_kernel, grid=(KV_HEADS,), in_specs=[q_spec, kv_sp...  15.8 us
    unnamed x125, local copies, waits for them, and re-layouts  15.1 us
    another operation x2, local copies, waits for them, and re-layouts, in_halves(): return padded(array.reshape(shape), axis + 1, to).reshape(flat)  10.9 us
    add x7, other arithmetic, total_of(): total = total + jnp.where(me == j, 0.0, received[j].astype(F32))  10.5 us
    pad x11, local copies, waits for them, and re-layouts, padded(): return jnp.pad(array, widths)  9.57 us

profile of v3, /device:TPU:0, one launch (start us, length us, event | category | flops | bytes accessed | tf_op | source)
XLA Modules:
  0.0 404.0 jit_solution(10898211372315967725)
XLA Ops:
  0.7 1.4 copy.49
  2.2 1.1 convert_element_type.452
  3.3 2.6 copy.51
  6.0 1.4 fusion.21
  8.1 3.6 pad.50.gu_in
  11.8 79.1 %shard_map.152 = (bf16[4,2,128,1600]{3,2,1,0:T(8,128)(2,1)}, bf16[4,2,128,960]{3,2,1,0:T(8,128)(2,1)}, bf16[4,2,128,1280]{3,2,1,0:T(8,128)(2,1)}, bf16[4,256,960...) custom-call(bf16[2,128,1600]{2,1,0:T(8,128)(2,1)S(1)} %pad.48.qkv_in, ...), custom_call_target="tpu_custom_call" | custom-call | flops 1000000000 | bytes 100000000 | tf_op jit(solution)/shard_map/pallas_call | solution.py:335
  90.9 2.2 slice.216
  94.4 1.0 copy-done.6
  96.3 25.4 %shard_map.153 = bf16[4,256,960]{2,1,0:T(8,128)(2,1)} custom-call(bf16[256,960]{1,0:T(8,128)(2,1)} %multiply_convert_fusion.3.refs_0_), custom_call_target="tpu_custom_call" | custom-call | bytes 39321600 | tf_op jit(solution)/shard_map/pallas_call | solution.py:182
  121.7 2.2 bitcast_dynamic-update-slice_fusion
  123.9 2.0 slice.217
  126.2 2.9 fusion.35
  129.2 4.6 %fusion.3 = (bf16[1024,640]{1,0:T(8,128)(2,1)}, bf16[1024,640]{1,0:T(8,128)(2,1)}, bf16[1024,640]{1,0:T(8,128)(2,1)}) fusion(f32[1024,1280]{1,0:T(8,128)S(1)} %fusion.35, bf16[1024,960]{1,0:T(8,128)(2,1)S(1)} %bitcast.219, bf16[640,960]{0,1:T(8,128)(2,1)S(1)} %copy-done), kind=kOutput, calls=%fused_computation.8 | convolution fusion | flops 1268776960 | bytes 12369920 | tf_op jit(solution)/shard_map/dot_general | solution.py:23
  133.7 4.2 %copy.58 = bf16[4,256,960]{1,0,2:T(4,128)(2,1)} copy(bf16[4,256,960]{2,1,0:T(8,128)(2,1)} %bitcast_dynamic-update-slice_fusion) | data formatting | bytes 3932160 | tf_op jit(solution)/shard_map/jit(dynamic_update_index_in_dim)/dynamic_update_slice | solution.py:525
  137.9 4.5 %reshape_reshape.7 = bf16[1024,16,60]{0,2,1:T(8,128)(2,1)} reshape(bf16[4,256,960]{1,0,2:T(4,128)(2,1)} %copy.58) | data formatting | bytes 3932160 | tf_op jit(solution)/shard_map/reshape;reshape | solution.py:414
  142.4 2.1 pad.53
  144.7 4.1 %convolution_convert_fusion.1.refs_2_ = bf16[1024,1280]{1,0:T(8,128)(2,1)} fusion(bf16[1024,1024]{0,1:T(8,128)(2,1)S(1)} %bitcast.220, bf16[1024,640]{1,0:T(8,128)(2,1)S(1)} %copy-done.58, bf16[1024,640]{1,0:T(8,128)(2,1)S(1)} %copy-done.56), kind=kOutput, calls=%fused_computation.2 | convolution fusion | flops 2690908160 | bytes 7340032 | tf_op jit(solution)/shard_map/dot_general | solution.py:23
  148.8 4.7 %reshape.551 = bf16[1024,2,480]{2,1,0:T(2,128)(2,1)} reshape(bf16[4,256,960]{2,1,0:T(8,128)(2,1)} %get-tuple-element.40) | data formatting | bytes 3932160 | tf_op jit(solution)/shard_map/reshape;reshape | solution.py:533
  153.5 6.2 %copy.70 = bf16[1024,2,480]{0,2,1:T(8,128)(2,1)} copy(bf16[1024,2,480]{2,1,0:T(2,128)(2,1)} %reshape.551) | data formatting | bytes 3932160 | tf_op jit(solution)/shard_map/reshape;reshape | solution.py:533
  159.7 1.8 pad.52
  161.6 2.6 convolution_convert_fusion.5.refs_1_
  164.3 4.0 convolution_convert_fusion.3
  168.3 3.9 copy.56
  172.1 25.7 %shard_map.154 = (bf16[4,256,960]{2,1,0:T(8,128)(2,1)}, bf16[2,640,512]{2,1,0:T(8,128)(2,1)}, bf16[2,1024,640]{2,1,0:T(8,128)(2,1)}) custom-call(bf16[4,256,960]{2,1,0:T(8,128)(2,1)} %bitcast.195, bf16[640,1024]{1,0:T(8,128)(2,1)} %convolution_convert_fusion.5.refs_1_, bf16[1024,1280]{1,0:T(8,128)(2,1)} %convolution_convert_fusion.1.refs_2_), custom_call_target="tpu_custom_call" | custom-call | bytes 117964800 | tf_op jit(solution)/shard_map/pallas_call | solution.py:182
  197.9 2.6 fusion.7
  200.5 3.4 fusion.12
  204.3 1.5 copy-done.17
  207.3 15.8 %shard_map.155 = (f32[960,256]{1,0:T(8,128)S(1)}, bf16[4,2,320,256]{3,2,1,0:T(8,128)(2,1)S(1)}) custom-call(bf16[960,256]{1,0:T(8,128)(2,1)S(1)} %get-tuple-element.38.q_ref, bf16[4,2,320,256]{3,2,1,0:T(8,128)(2,1)S(1)} %copy-done.5, bf16[960,256]{1,0:T(8,128)(2,1)S(1)} %convolution_convert_fusion.6.g_ref, f32[5,3,256]{2,1,0:T(4,128)S(1)} %get-tuple-element.42.lse_ref), custom_call_target="tpu_custom_call" | custom-call | flops 10066329600 | bytes 5242880 | tf_op jit(solution)/shard_map/pallas_call | solution.py:96
  223.2 1.1 copy-done.1
  225.2 3.1 convolution_convert_fusion.4
  228.3 3.9 copy.53
  232.1 43.7 %shard_map.156 = (bf16[4,640,256]{2,1,0:T(8,128)(2,1)}, bf16[4,256,960]{2,1,0:T(8,128)(2,1)}, bf16[4,160,512]{2,1,0:T(8,128)(2,1)}) custom-call(bf16[4,640,256]{2,1,0:T(8,128)(2,1)} %bitcast.190, bf16[4,256,960]{2,1,0:T(8,128)(2,1)} %bitcast.193, bf16[4,160,512]{2,1,0:T(8,128)(2,1)} %bitcast.209), custom_call_target="tpu_custom_call" | custom-call | bytes 78643200 | tf_op jit(solution)/shard_map/pallas_call | solution.py:182
  275.9 2.1 add_bitcast_fusion
  278.0 2.7 fusion.4
  280.8 1.3 copy.74
  282.9 1.4 add_add_fusion.3
  285.0 1.0 copy-done.11
  285.9 2.8 fusion.16
  288.8 1.4 stack.21
  290.2 1.4 stack.22
  293.6 1.0 pad.57
  294.6 1.1 reshape.527
  295.8 1.5 multiply_convert_fusion.2
  297.3 3.0 convolution_convert_fusion.refs_0_
  300.3 1.2 copy.61
  301.7 2.0 convolution_convert_fusion.2.refs_1_
  303.8 5.8 %shard_map.157 = (bf16[2,1024,896]{2,1,0:T(8,128)(2,1)}, bf16[2,1024,512]{2,1,0:T(8,128)(2,1)}, f32[2,4,4,8,128]{4,3,2,1,0:T(8,128)}) custom-call(bf16[1024,1792]{1,0:T(8,128)(2,1)} %convolution_convert_fusion.refs_0_, bf16[1024,1024]{1,0:T(8,128)(2,1)} %convolution_convert_fusion.2.refs_1_, f32[4,4,8,128]{3,2,1,0:T(8,128)} %pad.71.refs_2_), custom_call_target="tpu_custom_call" | custom-call | bytes 117964800 | tf_op jit(solution)/shard_map/pallas_call | solution.py:182
  309.6 1.5 bitcast_add_fusion.9.refs_2_
  311.1 3.4 fusion.6
  314.5 4.7 %fusion = bf16[1024,896]{1,0:T(8,128)(2,1)} fusion(bf16[2,1024,896]{2,1,0:T(8,128)(2,1)} %get-tuple-element.50, bf16[1024,1792]{1,0:T(8,128)(2,1)} %convolution_convert_fusion.refs_0_, s32[]{:T(128)S(6)} %select_n.555, pred[]{:T(512)S(6)} %eq.25, pred[]{:T(512)S(6)} %eq.24), kind=kLoop, calls=%fused_computation.4 | loop fusion | flops 7340032 | bytes 7340038 | tf_op jit(solution)/shard_map/convert_element_type | solution.py:468
  319.2 38.2 %shard_map.158 = (bf16[4,256,896]{2,1,0:T(8,128)(2,1)}, bf16[4,256,512]{2,1,0:T(8,128)(2,1)}, f32[4,4,8,128]{3,2,1,0:T(8,128)}, bf16[4,4,64,640]{3,2,1,0:T(8,128)(2,1)}) custom-call(bf16[4,256,896]{2,1,0:T(8,128)(2,1)} %bitcast.197, bf16[4,256,512]{2,1,0:T(8,128)(2,1)} %bitcast.203, f32[4,4,8,128]{3,2,1,0:T(8,128)} %bitcast_add_fusion.9.refs_2_, ...), custom_call_target="tpu_custom_call" | custom-call | bytes 85196800 | tf_op jit(solution)/shard_map/pallas_call | solution.py:182
  357.4 2.5 fusion.20.refs_3_
  359.9 2.2 add_convert_fusion.1
  362.1 2.2 add_convert_fusion
  364.4 1.3 select_add_fusion
  365.7 19.7 %shard_map.159 = (bf16[4,64,896]{2,1,0:T(8,128)(2,1)}, bf16[4,64,512]{2,1,0:T(8,128)(2,1)}, f32[4,8,128]{2,1,0:T(8,128)}, bf16[4,64,640]{2,1,0:T(8,128)(2,1)}) custom-call(bf16[4,64,896]{2,1,0:T(8,128)(2,1)} %bitcast.217, bf16[4,64,512]{2,1,0:T(8,128)(2,1)} %bitcast.227, f32[4,8,128]{2,1,0:T(8,128)} %bitcast.238, bf16[4,64,640]{2,1,0:T(8,128)(2,1)} %fusion.20.refs_3_), custom_call_target="tpu_custom_call" | custom-call | bytes 21299200 | tf_op jit(solution)/shard_map/pallas_call | solution.py:182
  385.4 1.5 dynamic-slice_dynamic-update-slice_fusion
  386.9 1.0 convert_bitcast_fusion
  389.5 1.8 add_bitcast_fusion.2
  391.3 1.7 add_bitcast_fusion.1
  394.2 1.6 fusion.10
  395.8 2.5 copy.66
  398.3 3.2 fusion.11
  401.5 2.5 copy.65
  (153 shorter events, 13.0 us)
Async XLA Ops:
  0.6 128.5 %copy-start = (bf16[640,960]{0,1:T(8,128)(2,1)S(1)}, bf16[640,960]{0,1:T(8,128)(2,1)}, u32[]{:S(2)}) copy-start(bf16[640,960]{0,1:T(8,128)(2,1)} %param.16) | copy-start | bytes 3686404
  0.6 1.6 copy-start.18
  2.0 3.9 copy-start.9
  2.0 3.9 copy-start.39
  2.2 1.1 copy-start.50
  2.2 3.8 copy-start.45
  3.3 4.3 %copy-start.53 = (s32[1,256]{1,0:T(1,128)S(1)}, s32[1,256]{1,0:T(1,128)}, u32[]{:S(2)}) copy-start(s32[1,256]{1,0:T(1,128)} %param.10) | copy-start | bytes 3076
  3.3 4.5 %copy-start.31 = (bf16[1,256,960]{1,2,0:T(8,128)(2,1)S(1)}, bf16[1,256,960]{1,2,0:T(8,128)(2,1)}, u32[]{:S(2)}) copy-start(bf16[1,256,960]{1,2,0:T(8,128)(2,1)} %param.17) | copy-start | bytes 1474564
  8.0 3.7 copy-start.29
  8.0 3.7 copy-start.30
  90.9 3.1 copy-start.4
  90.9 2.3 copy-start.10
  93.1 1.3 copy-start.16
  93.2 2.2 copy-start.36
  94.4 1.0 copy-start.6
  94.4 109.5 %copy-start.42 = (f32[256]{0:T(256)}, f32[256]{0:T(256)S(1)}, u32[]{:S(2)}) copy-start(f32[256]{0:T(256)S(1)} %fusion.30) | copy-start | bytes 3076
  123.9 2.3 copy-start.15
  125.9 3.2 copy-start.22
  126.2 2.9 copy-start.24
  142.4 2.2 copy-start.56
  142.4 2.3 copy-start.58
  159.7 1.9 copy-start.54
  161.6 2.6 copy-start.23
  161.6 2.7 copy-start.57
  161.6 2.7 copy-start.59
  200.5 3.4 copy-start.7
  203.9 2.7 copy-start.13
  203.9 1.9 copy-start.17
  203.9 2.7 copy-start.48
  205.8 0.8 copy-start.25
  205.8 1.5 copy-start.5
  207.3 17.8 %copy-start.55 = (bf16[1024,640]{1,0:T(8,128)(2,1)S(1)}, bf16[1024,640]{1,0:T(8,128)(2,1)}, u32[]{:S(2)}) copy-start(bf16[1024,640]{1,0:T(8,128)(2,1)} %get-tuple-element.93) | copy-start | bytes 3932164
  223.2 1.1 copy-start.1
  224.2 0.9 copy-start.2
  280.8 1.6 copy-start.3
  280.8 2.1 copy-start.27
  282.5 2.1 copy-start.21
  284.7 1.2 copy-start.11
  284.7 1.2 copy-start.40
  284.7 1.2 copy-start.46
  288.8 5.9 %copy-start.19 = (bf16[1,256,960]{1,2,0:T(8,128)(2,1)S(1)}, bf16[1,256,960]{1,2,0:T(8,128)(2,1)}, u32[]{:S(2)}) copy-start(bf16[1,256,960]{1,2,0:T(8,128)(2,1)} %param.9) | copy-start | bytes 1474564
  292.3 0.6 copy-start.34
  293.6 2.1 copy-start.41
  293.6 2.2 copy-start.47
  295.7 1.7 copy-start.20
  303.8 5.8 %copy-start.35 = (f32[4,4,2,60]{3,2,1,0:T(2,128)S(1)}, f32[4,4,2,60]{3,2,1,0:T(2,128)}, u32[]{:S(2)}) copy-start(f32[4,4,2,60]{3,2,1,0:T(2,128)} %copy-done.34) | copy-start | bytes 23044
  357.4 4.8 %copy-start.26 = (bf16[4,256,896]{2,1,0:T(8,128)(2,1)S(1)}, bf16[4,256,896]{2,1,0:T(8,128)(2,1)}, u32[]{:S(2)}) copy-start(bf16[4,256,896]{2,1,0:T(8,128)(2,1)} %get-tuple-element.54) | copy-start | bytes 5505028
  359.9 4.4 %copy-start.38 = (f32[4,4,8,128]{3,2,1,0:T(8,128)S(1)}, f32[4,4,8,128]{3,2,1,0:T(8,128)}, u32[]{:S(2)}) copy-start(f32[4,4,8,128]{3,2,1,0:T(8,128)} %get-tuple-element.53) | copy-start | bytes 196612
  387.9 1.5 copy-start.33
  388.0 3.3 copy-start.32
  388.0 6.2 %copy-start.28 = (f32[256,960]{1,0:T(8,128)S(1)}, f32[256,960]{1,0:T(8,128)}, u32[]{:S(2)}) copy-start(f32[256,960]{1,0:T(8,128)} %get-tuple-element.107) | copy-start | bytes 2949124
  388.4 4.6 %copy-start.44 = (f32[4,8,128]{2,1,0:T(8,128)S(1)}, f32[4,8,128]{2,1,0:T(8,128)}, u32[]{:S(2)}) copy-start(f32[4,8,128]{2,1,0:T(8,128)} %get-tuple-element.57) | copy-start | bytes 49156
  388.4 5.8 %copy-start.51 = (f32[256]{0:T(256)S(1)}, f32[256]{0:T(256)}, u32[]{:S(2)}) copy-start(f32[256]{0:T(256)} %copy-done.50) | copy-start | bytes 3076
  388.4 5.8 %copy-start.52 = (f32[256]{0:T(256)S(1)}, f32[256]{0:T(256)}, u32[]{:S(2)}) copy-start(f32[256]{0:T(256)} %get-tuple-element.87) | copy-start | bytes 3076
  388.4 5.8 %copy-start.8 = (f32[256,960]{1,0:T(8,128)S(1)}, f32[256,960]{1,0:T(8,128)}, u32[]{:S(2)}) copy-start(f32[256,960]{1,0:T(8,128)} %copy-done.6) | copy-start | bytes 2949124
  388.4 5.8 %copy-start.12 = (f32[1,256,960]{2,1,0:T(8,128)S(1)}, f32[1,256,960]{2,1,0:T(8,128)}, u32[]{:S(2)}) copy-start(f32[1,256,960]{2,1,0:T(8,128)} %copy-done.9) | copy-start | bytes 2949124
  388.4 5.8 %copy-start.14 = (f32[1,256,960]{2,1,0:T(8,128)S(1)}, f32[1,256,960]{2,1,0:T(8,128)}, u32[]{:S(2)}) copy-start(f32[1,256,960]{2,1,0:T(8,128)} %copy-done.13) | copy-start | bytes 2949124
  388.4 5.8 %copy-start.37 = (f32[960]{0:T(1024)S(1)}, f32[960]{0:T(1024)}, u32[]{:S(2)}) copy-start(f32[960]{0:T(1024)} %param.12) | copy-start | bytes 11524
  388.5 5.8 %copy-start.43 = (f32[256]{0:T(256)S(1)}, f32[256]{0:T(256)}, u32[]{:S(2)}) copy-start(f32[256]{0:T(256)} %copy-done.42) | copy-start | bytes 3076
  388.5 5.8 %copy-start.49 = (f32[256]{0:T(256)S(1)}, f32[256]{0:T(256)}, u32[]{:S(2)}) copy-start(f32[256]{0:T(256)} %copy-done.48) | copy-start | bytes 3076

commit v4 on v3

--- a/solution.py
+++ b/solution.py
@@ -55,58 +55,6 @@
     key_at = lax.broadcasted_iota(jnp.int32, (keys, rows), 0)
     row_at = lax.broadcasted_iota(jnp.int32, (keys, rows), 1)
     return key_at <= row_at + start
-
-
-def backward_kernel(q_ref, kv_ref, g_ref, lse_ref, dq_ref, dkv_ref):
-    rows = q_ref.shape[1]
-    kv = kv_ref[...]
-    parts = kv.shape[0]
-    keys, keys_t = keys_first(kv, 0)
-    values, _ = keys_first(kv, 1)
-    allowed = allowed_of(keys.shape[0], rows)
-    dk = jnp.zeros((HD, keys.shape[0]), F32)
-    dv = jnp.zeros((HD, keys.shape[0]), F32)
-    for h in range(GROUP):
-        q = q_ref[h * HD : (h + 1) * HD, :]
-        g = g_ref[h * HD : (h + 1) * HD, :]
-        scores = jnp.where(allowed, dot(keys, q, 1, 0), -1e30)
-        prob = jnp.exp(scores - lse_ref[0, h : h + 1, :])
-        dprob = dot(values, g, 1, 0)
-        inner = jnp.sum(dprob * prob, axis=0, keepdims=True)
-        ds = (prob * (dprob - inner)).astype(BF16)
-        dq_ref[h * HD : (h + 1) * HD, :] = dot(keys_t, ds, 1, 0) * (HD**-0.5)
-        dk = dk + dot(q, ds, 1, 1)
-        dv = dv + dot(g, prob.astype(BF16), 1, 1)
-    for c in range(parts):
-        dkv_ref[c, 0] = dk[:, c * rows : (c + 1) * rows].astype(BF16)
-        dkv_ref[c, 1] = dv[:, c * rows : (c + 1) * rows].astype(BF16)
-
-
-def attention_specs(parts, rows):
-    q_spec = pl.BlockSpec((GROUP * HD, rows), lambda g: (g, 0))
-    kv_spec = pl.BlockSpec((parts, 2, HD, rows), lambda g: (0, 0, g, 0))
-    lse_spec = pl.BlockSpec((1, GROUP, rows), lambda g: (g, 0, 0))
-    return q_spec, kv_spec, lse_spec
-
-
-def attention_backward(q, kv, g, lse):
-    parts, rows = kv.shape[0], q.shape[1]
-    q_spec, kv_spec, lse_spec = attention_specs(parts, rows)
-    work = parts * rows * rows * HD * HEADS
-    return pl.pallas_call(
-        backward_kernel,
-        grid=(KV_HEADS,),
-        in_specs=[q_spec, kv_spec, q_spec, lse_spec],
-        out_specs=[q_spec, kv_spec],
-        out_shape=[
-            jax.ShapeDtypeStruct((D, rows), F32),
-            jax.ShapeDtypeStruct(kv.shape, BF16),
-        ],
-        compiler_params=pltpu.CompilerParams(vmem_limit_bytes=40 * 2**20),
-        cost_estimate=pl.CostEstimate(
-            flops=40 * work, bytes_accessed=5 * 2**20, transcendentals=work // HD
-        ),
-    )(q, kv, g, lse)
 
 
 MESH = pl.DeviceIdType.MESH
@@ -363,6 +311,102 @@
     )(qkv_in, out_in, gu_in, cot_in, normed, cosine, sine)
 
 
+def back_kernel(
+    q_ref, kv, g_ref, lse_ref, down_in, dq_ref, dkv, kv_out, down_out,
+    down_send, down_recv, kv_send, kv_recv,
+):
+    fsdp, ctx = lax.axis_size("fsdp"), lax.axis_size("ctx")
+    me, here = lax.axis_index("fsdp"), lax.axis_index("ctx")
+    rows = q_ref.shape[1]
+    greet(("fsdp", "ctx"))
+    downs = [
+        send(
+            down_in.at[peer_of("fsdp", k)], down_out.at[me], (down_send, down_recv), k - 1, "fsdp", k
+        )
+        for k in range(1, fsdp)
+    ]
+    allowed = allowed_of(ctx * rows, rows)
+
+    def kv_copy(g, k):
+        at = pl.ds(pl.multiple_of(g * HD, HD), HD)
+        spot = g * (ctx - 1) + k - 1
+        there = peer_of("ctx", k)
+        return pltpu.make_async_remote_copy(
+            src_ref=dkv.at[there, :, at, :],
+            dst_ref=kv_out.at[here, :, at, :],
+            send_sem=kv_send.at[spot],
+            recv_sem=kv_recv.at[spot],
+            device_id={"ctx": there},
+            device_id_type=MESH,
+        )
+
+    def attend_back(g, carry):
+        at = pl.ds(pl.multiple_of(g * HD, HD), HD)
+        keys = jnp.concatenate([kv[c, 0, at, :].T for c in range(ctx)], axis=0)
+        keys_t = jnp.concatenate([kv[c, 0, at, :] for c in range(ctx)], axis=1)
+        values = jnp.concatenate([kv[c, 1, at, :].T for c in range(ctx)], axis=0)
+        dk = jnp.zeros((HD, ctx * rows), F32)
+        dv = jnp.zeros((HD, ctx * rows), F32)
+        for h in range(GROUP):
+            spot = pl.ds(pl.multiple_of((g * GROUP + h) * HD, HD), HD)
+            q, grad = q_ref[spot, :], g_ref[spot, :]
+            scores = jnp.where(allowed, dot(keys, q, 1, 0), -1e30)
+            prob = jnp.exp(scores - lse_ref[g, h : h + 1, :])
+            dprob = dot(values, grad, 1, 0)
+            inner = jnp.sum(dprob * prob, axis=0, keepdims=True)
+            ds = (prob * (dprob - inner)).astype(BF16)
+            dq_ref[spot, :] = dot(keys_t, ds, 1, 0) * (HD**-0.5)
+            dk = dk + dot(q, ds, 1, 1)
+            dv = dv + dot(grad, prob.astype(BF16), 1, 1)
+        for c in range(ctx):
+            dkv[c, 0, at, :] = dk[:, c * rows : (c + 1) * rows].astype(BF16)
+            dkv[c, 1, at, :] = dv[:, c * rows : (c + 1) * rows].astype(BF16)
+        for k in range(1, ctx):
+            kv_copy(g, k).start()
+        return carry
+
+    def finish(g, carry):
+        for k in range(1, ctx):
+            kv_copy(g, k).wait()
+        return carry
+
+    lax.fori_loop(0, KV_HEADS, attend_back, 0)
+    lax.fori_loop(0, KV_HEADS, finish, 0)
+    for copy in downs:
+        copy.wait()
+
+
+def back(q, kv, g, lse, down_part):
+    parts, rows = kv.shape[0], q.shape[1]
+    fsdp = down_part.shape[0]
+    work = parts * rows * rows * HD * HEADS
+    anywhere, vmem = pl.BlockSpec(memory_space=pl.ANY), pl.BlockSpec(memory_space=pltpu.VMEM)
+    shape = jax.ShapeDtypeStruct
+    return pl.pallas_call(
+        back_kernel,
+        in_specs=[vmem] * 4 + [anywhere],
+        out_specs=[vmem] * 3 + [anywhere],
+        out_shape=[
+            shape((D, rows), F32),
+            shape(kv.shape, BF16),
+            shape(kv.shape, BF16),
+            shape(down_part.shape, BF16),
+        ],
+        scratch_shapes=[
+            pltpu.SemaphoreType.DMA((fsdp - 1,)),
+            pltpu.SemaphoreType.DMA((fsdp - 1,)),
+            pltpu.SemaphoreType.DMA((KV_HEADS * (parts - 1),)),
+            pltpu.SemaphoreType.DMA((KV_HEADS * (parts - 1),)),
+        ],
+        compiler_params=pltpu.CompilerParams(
+            collective_id=3, has_side_effects=True, vmem_limit_bytes=48 * 2**20
+        ),
+        cost_estimate=pl.CostEstimate(
+            flops=40 * work, bytes_accessed=5 * 2**20, transcendentals=work // HD
+        ),
+    )(q, kv, g, lse, down_part)
+
+
 def padded(array, axis, to):
     widths = [(0, 0)] * array.ndim
     widths[axis] = (0, to - array.shape[axis])
@@ -415,20 +459,17 @@
         return padded(array, 2, pad).reshape(-1, fsdp * ctx * pad)
 
     grad_gu = dot(spread(two_all), grad_gate_up, 0, 0).astype(BF16)
+    grad_down = grad_down.reshape(ctx, part // ctx, -1)
     if dp == 2:
         two_sum, down_grads, gu_sum = swap(
-            2,
-            (two_part, "fsdp", "rows"),
-            (grad_down, "dp", "columns"),
-            (grad_gu, "dp", "columns"),
+            2, (two_part, "fsdp", "rows"), (grad_down, "ctx", "rows"), (grad_gu, "dp", "columns")
         )
         gu_cols = total_of(gu_sum, grad_gu, "dp", "columns").astype(BF16)
     else:
-        two_sum, down_grads = swap(2, (two_part, "fsdp", "rows"), (grad_down, "dp", "columns"))
+        two_sum, down_grads = swap(2, (two_part, "fsdp", "rows"), (grad_down, "ctx", "rows"))
         gu_cols = grad_gu
     grad_two = total_of(two_sum, two_part, "fsdp", "rows")
-    down_grads = total_of(down_grads, grad_down, "dp", "columns").astype(BF16)
-    down_grads = down_grads.reshape(ctx, part // ctx, -1)
+    down_grads = total_of(down_grads, grad_down, "ctx", "rows").astype(BF16)
     gu_cols = gu_cols.reshape(fsdp, ctx, pad, -1).transpose(1, 0, 2, 3)
 
     grad_rows = cotangent[0].astype(F32)
@@ -439,14 +480,11 @@
     grad_attended = dot(full_out, grad_attn, 1, 1).astype(BF16)
     attended_wide = padded(attended.reshape(fsdp * ctx, slim, rows), 1, pad).reshape(-1, rows)
     grad_out = dot(attended_wide, in_halves(grad_attn, 1, dp), 1, 0).astype(BF16)
-    grad_queries, kv_grads = attention_backward(queries, every_kv, grad_attended, lse)
-    kv_grads = kv_grads.reshape(ctx, 2 * KVW, rows)
-    kv_sum, down_sum, last_down = swap(
-        3, (kv_grads, "ctx", "rows"), (down_part, "fsdp", "rows"), (down_grads, "ctx", "rows")
-    )
-    own_kv = total_of(kv_sum, kv_grads, "ctx", "rows")
+    grad_queries, kv_grads, kv_sum, down_sum = back(
+        queries, every_kv, grad_attended, lse, down_part
+    )
+    own_kv = total_of(kv_sum, kv_grads, "ctx", "rows").reshape(2 * KVW, rows)
     outputs = hidden + total_of(down_sum, down_part, "fsdp", "rows")
-    result_down = total_of(last_down, down_grads, "ctx", "rows")[:, : D // dp]
     grad_project = jnp.concatenate(
         [
             rotate(grad_queries, cosine, -sine),
@@ -463,7 +501,14 @@
 
     gains = jnp.stack([grad_gain_attn, grad_gain_mlp]).reshape(2, fsdp, ctx, slim)
     gains = padded(padded(gains.transpose(1, 2, 0, 3), 2, 8), 3, 128)
-    arrived = swap(4, (grad_qkv, "dp", "columns"), (grad_out, "dp", "columns"), (gains, "dp", "all"))
+    arrived = swap(
+        4,
+        (grad_qkv, "dp", "columns"),
+        (grad_out, "dp", "columns"),
+        (gains, "dp", "all"),
+        (down_grads, "dp", "columns"),
+    )
+    result_down = total_of(arrived[3], down_grads, "dp", "columns")[:, : D // dp]
     sent = [
         total_of(arrived[0], grad_qkv, "dp", "columns").astype(BF16).reshape(fsdp, ctx * pad, -1),
         total_of(arrived[1], grad_out, "dp", "columns").astype(BF16).reshape(fsdp, ctx * pad, -1),

time: 406 us -> 383 us (0.943)
  Pallas kernels: 253 us -> 232 us
  other arithmetic: 49.1 us -> 43.6 us
    pallas_call x6 -> x5, Pallas kernels: 158 us -> 114 us  [swap(): pl.pallas_call(functools.partial(swap_kernel, plan), in_specs=[pl.BlockSp...]
    pallas_call x1, Pallas kernels: 15.8 us -> 39.3 us  [back(): pl.pallas_call(back_kernel, in_specs=[vmem] * 4 + [anywhere], out_specs=[...]
    unnamed x125 -> x93, local copies, waits for them, and re-layouts: 15.1 us -> 19.3 us
where the time goes in v4:
time: 383 us; the launch traced here: 381 us
  Pallas kernels  232 us (61%)
  local copies, waits for them, and re-layouts  72.7 us (19%)
  other arithmetic  43.6 us (11%)
  matrix products  31.4 us (8%)
    pallas_call x5, Pallas kernels, swap(): pl.pallas_call(functools.partial(swap_kernel, plan), in_specs=[pl.BlockSp...  114 us
    pallas_call x1, Pallas kernels, front(): pl.pallas_call(functools.partial(front_kernel, dp == 2), in_specs=[anywhe...  79 us
    pallas_call x1, Pallas kernels, back(): pl.pallas_call(back_kernel, in_specs=[vmem] * 4 + [anywhere], out_specs=[...  39.3 us
    dot_general x11, matrix products, dot(): lax.dot_general(a, b, (((ca,), (cb,)), ((), ())), preferred_element_type=...  31.4 us
    unnamed x93, local copies, waits for them, and re-layouts  19.3 us
    another operation x2, local copies, waits for them, and re-layouts, in_halves(): return padded(array.reshape(shape), axis + 1, to).reshape(flat)  10.9 us
    pad x11, local copies, waits for them, and re-layouts, padded(): return jnp.pad(array, widths)  9.09 us
    add x7, other arithmetic, total_of(): total = total + jnp.where(me == j, 0.0, received[j].astype(F32))  8.51 us

profile of v4, /device:TPU:0, one launch (start us, length us, event | category | flops | bytes accessed | tf_op | source)
XLA Modules:
  0.0 381.2 jit_solution(18066283133916435691)
XLA Ops:
  0.7 1.4 pad.48.qkv_in
  2.0 1.1 pad.49.out_in
  3.1 1.8 pad.50.gu_in
  4.9 1.2 copy.50
  6.1 2.0 convert_element_type.452
  8.2 2.5 copy.51
  10.8 2.2 copy.49
  13.0 1.4 fusion.12
  14.4 1.4 fusion.20
  16.2 79.0 %shard_map.152 = (bf16[4,2,128,1600]{3,2,1,0:T(8,128)(2,1)}, bf16[4,2,128,960]{3,2,1,0:T(8,128)(2,1)}, bf16[4,2,128,1280]{3,2,1,0:T(8,128)(2,1)}, bf16[4,256,960...) custom-call(bf16[2,128,1600]{2,1,0:T(8,128)(2,1)S(1)} %pad.48.qkv_in, ...), custom_call_target="tpu_custom_call" | custom-call | flops 1000000000 | bytes 100000000 | tf_op jit(solution)/shard_map/pallas_call | solution.py:283
  95.2 2.5 slice.220
  99.1 1.6 copy-done.24
  100.6 1.6 slice.221
  103.2 25.4 %shard_map.153 = bf16[4,256,960]{2,1,0:T(8,128)(2,1)} custom-call(bf16[256,960]{1,0:T(8,128)(2,1)} %multiply_convert_fusion.3.refs_0_), custom_call_target="tpu_custom_call" | custom-call | bytes 39321600 | tf_op jit(solution)/shard_map/pallas_call | solution.py:130
  128.6 1.0 bitcast_dynamic-update-slice_fusion
  129.6 5.3 %fusion.34 = f32[1024,1280]{1,0:T(8,128)S(1)} fusion(bf16[1024,960]{1,0:T(8,128)(2,1)} %bitcast.187, bf16[960,1280]{1,0:T(8,128)(2,1)} %bitcast.203), kind=kOutput, calls=%fused_computation.102 | convolution fusion | flops 2516582400 | bytes 9666560 | tf_op jit(solution)/shard_map/dot_general | solution.py:23
  134.9 3.6 fusion.3
  138.5 1.1 copy-done.40
  140.0 4.0 %convolution_convert_fusion.3 = bf16[1024,960]{0,1:T(8,128)(2,1)} fusion(bf16[960,1280]{1,0:T(8,128)(2,1)S(1)} %bitcast.204, bf16[1024,640]{1,0:T(8,128)(2,1)S(1)} %get-tuple-element.92, bf16[1024,640]{1,0:T(8,128)(2,1)S(1)} %get-tuple-element.91), kind=kOutput, calls=%fused_computation.21 | convolution fusion | flops 2522808320 | bytes 7045120 | tf_op jit(solution)/shard_map/dot_general | solution.py:23
  144.0 3.9 %copy.56 = bf16[1024,960]{1,0:T(8,128)(2,1)} copy(bf16[1024,960]{0,1:T(8,128)(2,1)} %convolution_convert_fusion.3) | data formatting | bytes 3932160 | tf_op jit(solution)/shard_map/convert_element_type | solution.py:453
  147.9 4.7 %reshape.557 = bf16[1024,2,480]{2,1,0:T(2,128)(2,1)} reshape(bf16[4,256,960]{2,1,0:T(8,128)(2,1)} %get-tuple-element.40) | data formatting | bytes 3932160 | tf_op jit(solution)/shard_map/reshape;reshape | solution.py:578
  152.5 6.2 %copy.70 = bf16[1024,2,480]{0,2,1:T(8,128)(2,1)} copy(bf16[1024,2,480]{2,1,0:T(2,128)(2,1)} %reshape.557) | data formatting | bytes 3932160 | tf_op jit(solution)/shard_map/reshape;reshape | solution.py:578
  158.8 1.8 pad.52
  160.7 2.6 convolution_convert_fusion.5
  163.3 4.2 %copy.58 = bf16[4,256,960]{1,0,2:T(4,128)(2,1)} copy(bf16[4,256,960]{2,1,0:T(8,128)(2,1)} %bitcast_dynamic-update-slice_fusion) | data formatting | bytes 3932160 | tf_op jit(solution)/shard_map/jit(dynamic_update_index_in_dim)/dynamic_update_slice | solution.py:570
  167.5 4.5 %reshape_reshape.7 = bf16[1024,16,60]{0,2,1:T(8,128)(2,1)} reshape(bf16[4,256,960]{1,0,2:T(4,128)(2,1)} %copy.58) | data formatting | bytes 3932160 | tf_op jit(solution)/shard_map/reshape;reshape | solution.py:458
  172.0 2.1 pad.53
  174.4 4.2 %convolution_convert_fusion.1.refs_2_ = bf16[1024,1280]{1,0:T(8,128)(2,1)} fusion(bf16[1024,1024]{0,1:T(8,128)(2,1)S(1)} %bitcast.208, bf16[1024,640]{1,0:T(8,128)(2,1)S(1)} %copy-done.43, bf16[1024,640]{1,0:T(8,128)(2,1)S(1)} %copy-done.41), kind=kOutput, calls=%fused_computation.2 | convolution fusion | flops 2690908160 | bytes 7340032 | tf_op jit(solution)/shard_map/dot_general | solution.py:23
  178.6 26.6 %shard_map.154 = (bf16[4,256,960]{2,1,0:T(8,128)(2,1)}, bf16[4,160,1024]{2,1,0:T(8,128)(2,1)}, bf16[2,1024,640]{2,1,0:T(8,128)(2,1)}) custom-call(bf16[4,256,960]{2,1,0:T(8,128)(2,1)} %bitcast.183, bf16[4,160,1024]{2,1,0:T(8,128)(2,1)} %bitcast.213, bf16[1024,1280]{1,0:T(8,128)(2,1)} %convolution_convert_fusion.1.refs_2_), custom_call_target="tpu_custom_call" | custom-call | bytes 117964800 | tf_op jit(solution)/shard_map/pallas_call | solution.py:130
  205.1 2.4 fusion.11
  207.9 1.6 copy-done.19
  209.5 1.5 convolution_convert_fusion.6.g_ref
  211.0 3.0 convolution_convert_fusion.4
  214.0 3.9 %copy.53 = bf16[1024,960]{1,0:T(8,128)(2,1)} copy(bf16[1024,960]{0,1:T(8,128)(2,1)} %convolution_convert_fusion.4) | data formatting | bytes 3932160 | tf_op jit(solution)/shard_map/convert_element_type | solution.py:454
  217.9 1.3 copy-done.6
  219.2 1.0 copy-done.8
  220.2 1.0 copy-done.9
  221.3 39.3 %shard_map.155 = (f32[960,256]{1,0:T(8,128)S(1)}, bf16[4,2,320,256]{3,2,1,0:T(8,128)(2,1)S(1)}, bf16[4,2,320,256]{3,2,1,0:T(8,128)(2,1)S(1)}, bf16[4,256,960]{2,1,0:T(8,128)(2,1)}) custom-call(bf16[960,256]{1,0:T(8,128)(2,1)S(1)} %copy-done.8, bf16[4,2,320,256]{3,2,1,0:T(8,128)(2,1)S(1)} %copy-done.6, bf16[960,256]{1,0:T(8,128)(2,1)S(1)} %copy-done.9, ...), custom_call_target="tpu_custom_call" | custom-call | flops 10066329600 | bytes 5242880 | tf_op jit(solution)/shard_map/pallas_call | solution.py:385
  260.6 1.0 copy-done.4
  261.6 3.2 fusion.10
  264.8 2.5 copy.65
  267.3 3.8 slice.243
  271.1 1.3 add_add_fusion.3
  272.7 1.6 copy-done.21
  274.6 1.3 fusion.15
  276.7 1.3 copy.66
  279.0 3.0 convolution_convert_fusion.refs_0_
  283.3 2.0 convolution_convert_fusion.2.refs_1_
  286.2 2.4 add_convert_fusion.1
  288.6 6.0 %shard_map.156 = (bf16[2,1024,896]{2,1,0:T(8,128)(2,1)}, bf16[2,1024,512]{2,1,0:T(8,128)(2,1)}, f32[2,4,4,8,128]{4,3,2,1,0:T(8,128)}, bf16[2,160,512]{2,1,0:T(8,128)(2,1)}) custom-call(bf16[1024,1792]{1,0:T(8,128)(2,1)} %convolution_convert_fusion.refs_0_, bf16[1024,1024]{1,0:T(8,128)(2,1)} %convolution_convert_fusion.2.refs_1_, ...), custom_call_target="tpu_custom_call" | custom-call | bytes 124518400 | tf_op jit(solution)/shard_map/pallas_call | solution.py:130
  294.7 4.9 %fusion = bf16[1024,896]{1,0:T(8,128)(2,1)} fusion(bf16[2,1024,896]{2,1,0:T(8,128)(2,1)} %get-tuple-element.50, bf16[1024,1792]{1,0:T(8,128)(2,1)} %convolution_convert_fusion.refs_0_, s32[]{:T(128)S(6)} %select_n.558, pred[]{:T(512)S(6)} %eq.29, pred[]{:T(512)S(6)} %eq.28), kind=kLoop, calls=%fused_computation.4 | loop fusion | flops 7340032 | bytes 7340038 | tf_op jit(solution)/shard_map/convert_element_type | solution.py:513
  299.6 3.1 fusion.6
  303.3 2.7 fusion.4
  306.1 1.2 copy.74
  307.3 36.5 %shard_map.157 = (bf16[4,256,896]{2,1,0:T(8,128)(2,1)}, bf16[4,256,512]{2,1,0:T(8,128)(2,1)}, f32[4,4,8,128]{3,2,1,0:T(8,128)}, bf16[4,4,64,640]{3,2,1,0:T(8,128)(2,1)}) custom-call(bf16[4,256,896]{2,1,0:T(8,128)(2,1)} %bitcast.185, bf16[4,256,512]{2,1,0:T(8,128)(2,1)} %bitcast.191, f32[4,4,8,128]{3,2,1,0:T(8,128)} %bitcast_add_fusion.7.refs_2_, ...), custom_call_target="tpu_custom_call" | custom-call | bytes 85196800 | tf_op jit(solution)/shard_map/pallas_call | solution.py:130
  343.8 1.5 select_add_fusion
  345.3 2.8 add_convert_fusion
  348.1 1.9 add_convert_fusion.2
  350.0 2.0 fusion.19.refs_3_
  352.0 19.4 %shard_map.158 = (bf16[4,64,896]{2,1,0:T(8,128)(2,1)}, bf16[4,64,512]{2,1,0:T(8,128)(2,1)}, f32[4,8,128]{2,1,0:T(8,128)}, bf16[4,64,640]{2,1,0:T(8,128)(2,1)}) custom-call(bf16[4,64,896]{2,1,0:T(8,128)(2,1)} %bitcast.205, bf16[4,64,512]{2,1,0:T(8,128)(2,1)} %bitcast.218, f32[4,8,128]{2,1,0:T(8,128)} %bitcast.229, bf16[4,64,640]{2,1,0:T(8,128)(2,1)} %fusion.19.refs_3_), custom_call_target="tpu_custom_call" | custom-call | bytes 21299200 | tf_op jit(solution)/shard_map/pallas_call | solution.py:130
  372.7 1.9 add_bitcast_fusion.1
  374.6 1.7 add_bitcast_fusion.2
  376.3 1.5 dynamic-slice_dynamic-update-slice_fusion
  377.8 1.1 convert_bitcast_fusion
  (120 shorter events, 12.3 us)
Async XLA Ops:
  0.6 134.3 %copy-start = (bf16[640,960]{0,1:T(8,128)(2,1)S(1)}, bf16[640,960]{0,1:T(8,128)(2,1)}, u32[]{:S(2)}) copy-start(bf16[640,960]{0,1:T(8,128)(2,1)} %param.16) | copy-start | bytes 3686404
  0.7 2.5 copy-start.22
  4.9 5.8 %copy-start.36 = (f32[960]{0:T(1024)S(1)}, f32[960]{0:T(1024)}, u32[]{:S(2)}) copy-start(f32[960]{0:T(1024)} %param.11) | copy-start | bytes 11524
  13.0 3.0 copy-start.37
  95.2 3.5 copy-start.2
  95.2 3.5 copy-start.5
  95.2 3.5 copy-start.7
  95.2 2.6 copy-start.13
  97.8 1.3 copy-start.18
  97.9 2.8 copy-start.24
  99.1 108.5 %copy-start.10 = (f32[256,960]{1,0:T(8,128)}, f32[256,960]{1,0:T(8,128)S(1)}, u32[]{:S(2)}) copy-start(f32[256,960]{1,0:T(8,128)S(1)} %get-tuple-element.106) | copy-start | bytes 2949124
  100.6 1.6 copy-start.35
  129.6 5.4 %copy-start.25 = (bf16[4,256,960]{2,1,0:T(8,128)(2,1)S(1)}, bf16[4,256,960]{2,1,0:T(8,128)(2,1)}, u32[]{:S(2)}) copy-start(bf16[4,256,960]{2,1,0:T(8,128)(2,1)} %get-tuple-element.40) | copy-start | bytes 5898244
  134.9 5.1 %copy-start.23 = (bf16[4,2,120,1280]{3,2,1,0:T(8,128)(2,1)S(1)}, bf16[4,2,120,1280]{3,2,1,0:T(8,128)(2,1)}, u32[]{:S(2)}) copy-start(bf16[4,2,120,1280]{3,2,1,0:T(8,128)(2,1)} %slice.221) | copy-start | bytes 7372804
  138.5 1.1 copy-start.40
  138.5 1.5 copy-start.42
  158.8 1.9 copy-start.38
  172.0 2.2 copy-start.41
  172.0 2.3 copy-start.43
  207.5 3.4 copy-start.16
  207.5 1.9 copy-start.19
  209.5 1.5 copy-start.26
  209.5 1.5 copy-start.39
  217.9 1.3 copy-start.6
  219.2 1.0 copy-start.8
  220.2 1.0 copy-start.9
  221.3 40.3 %copy-start.11 = (f32[256,960]{1,0:T(8,128)S(1)}, f32[256,960]{1,0:T(8,128)}, u32[]{:S(2)}) copy-start(f32[256,960]{1,0:T(8,128)} %copy-done.10) | copy-start | bytes 2949124
  260.5 1.0 copy-start.4
  272.3 2.0 copy-start.21
  272.4 2.2 copy-start.14
  272.5 3.4 copy-start.31
  274.6 1.4 copy-start.12
  274.6 1.5 copy-start.17
  276.6 1.3 copy-start.20
  277.9 0.9 copy-start.32
  279.0 3.0 copy-start.3
  282.0 1.0 copy-start.27
  294.6 4.9 %copy-start.15 = (bf16[1024,1024]{1,0:T(8,128)(2,1)S(1)}, bf16[1024,1024]{1,0:T(8,128)(2,1)}, u32[]{:S(2)}) copy-start(bf16[1024,1024]{1,0:T(8,128)(2,1)} %convolution_convert_fusion.2.refs_1_) | copy-start | bytes 6291460
  299.6 3.1 copy-start.34
  343.8 4.4 %copy-start.30 = (bf16[4,256,512]{2,1,0:T(8,128)(2,1)S(1)}, bf16[4,256,512]{2,1,0:T(8,128)(2,1)}, u32[]{:S(2)}) copy-start(bf16[4,256,512]{2,1,0:T(8,128)(2,1)} %get-tuple-element.55) | copy-start | bytes 3145732
  345.3 4.8 %copy-start.29 = (bf16[4,4,64,640]{3,2,1,0:T(8,128)(2,1)S(1)}, bf16[4,4,64,640]{3,2,1,0:T(8,128)(2,1)}, u32[]{:S(2)}) copy-start(bf16[4,4,64,640]{3,2,1,0:T(8,128)(2,1)} %get-tuple-element.56) | copy-start | bytes 3932164
  377.8 3.4 copy-start.1
  378.9 1.4 copy-start.28
  379.0 1.4 copy-start.33

commit v5 on v4

--- a/solution.py
+++ b/solution.py
@@ -421,6 +421,7 @@
     slim = D // (fsdp * ctx)
     half, wide_half = own // 2, -(-own // 2 // 128) * 128
     pad = -(-slim // 16) * 16
+    wide = w_qkv.shape[1] // dp
     inputs = tokens[0].astype(F32)
     cosine, sine = angles_of(positions[0])
     normed = normalize(inputs, gain_attn).astype(BF16)
@@ -510,29 +511,31 @@
     )
     result_down = total_of(arrived[3], down_grads, "dp", "columns")[:, : D // dp]
     sent = [
-        total_of(arrived[0], grad_qkv, "dp", "columns").astype(BF16).reshape(fsdp, ctx * pad, -1),
-        total_of(arrived[1], grad_out, "dp", "columns").astype(BF16).reshape(fsdp, ctx * pad, -1),
+        jnp.concatenate(
+            [
+                total_of(arrived[0], grad_qkv, "dp", "columns")[:, :wide],
+                total_of(arrived[1], grad_out, "dp", "columns")[:, : D // dp],
+            ],
+            axis=1,
+        ).astype(BF16).reshape(fsdp, ctx * pad, -1),
         total_of(arrived[2], gains, "dp", "all"),
         gu_cols,
     ]
     arrived = swap(
-        5, *[(x, axis, "rows") for x, axis in zip(sent, ("fsdp", "fsdp", "fsdp", "ctx"))]
+        5, *[(x, axis, "rows") for x, axis in zip(sent, ("fsdp", "fsdp", "ctx"))]
     )
     sent = [
         total_of(arrived[0], sent[0], "fsdp", "rows").astype(BF16).reshape(ctx, pad, -1),
-        total_of(arrived[1], sent[1], "fsdp", "rows").astype(BF16).reshape(ctx, pad, -1),
-        total_of(arrived[2], sent[2], "fsdp", "rows"),
-        total_of(arrived[3], sent[3], "ctx", "rows").astype(BF16),
+        total_of(arrived[1], sent[1], "fsdp", "rows"),
+        total_of(arrived[2], sent[2], "ctx", "rows").astype(BF16),
     ]
     arrived = swap(
-        6, *[(x, axis, "rows") for x, axis in zip(sent, ("ctx", "ctx", "ctx", "fsdp"))]
-    )
-    result_qkv, result_out, gains = [
-        total_of(arrived[i], sent[i], "ctx", "rows") for i in range(3)
-    ]
+        6, *[(x, axis, "rows") for x, axis in zip(sent, ("ctx", "ctx", "fsdp"))]
+    )
+    both, gains = [total_of(arrived[i], sent[i], "ctx", "rows") for i in range(2)]
     gains = gains[:2, :slim]
-    own_gu = lax.dynamic_index_in_dim(sent[3], lax.axis_index("fsdp"), 0, keepdims=False)
-    gu_rows = with_own(arrived[3], own_gu, "fsdp")
+    own_gu = lax.dynamic_index_in_dim(sent[2], lax.axis_index("fsdp"), 0, keepdims=False)
+    gu_rows = with_own(arrived[2], own_gu, "fsdp")
     gu_rows = gu_rows[:, :slim]
     if dp == 2:
         result_gu = gu_rows.transpose(1, 0, 2).reshape(slim, FF)
@@ -544,8 +547,8 @@
         grad_inputs[None],
         gains[0],
         gains[1],
-        result_qkv[:slim, : w_qkv.shape[1] // dp],
-        result_out[:slim, : D // dp],
+        both[:slim, :wide],
+        both[:slim, wide:],
         result_gu.astype(F32),
         result_down,
     )

time: 383 us -> 401 us (1.047); the launches traced: 381 us -> 395 us
  other arithmetic: 43.6 us -> 49.9 us
  Pallas kernels: 232 us -> 238 us
    convert_element_type x4 -> x1, other arithmetic: 11.9 us -> 1.99 us  [shards(): total_of(arrived[2], sent[2], 'ctx', 'rows').astype(BF16)]
    pallas_call x1, Pallas kernels: 39.3 us -> 49.1 us  [back(): pl.pallas_call(back_kernel, in_specs=[vmem] * 4 + [anywhere], out_specs=[...]
    another operation x0 -> x2, other arithmetic: none -> 8.16 us
    select_n x0 -> x2, other arithmetic: none -> 7.73 us  [total_of(): total = total + jnp.where(me == j, 0.0, received[j].astype(F32))]
    pallas_call x5, Pallas kernels: 114 us -> 109 us  [swap(): pl.pallas_call(functools.partial(swap_kernel, plan), in_specs=[pl.BlockSp...]
    add x7 -> x6, other arithmetic: 8.51 us -> 6.21 us  [total_of(): total = total + jnp.where(me == j, 0.0, received[j].astype(F32))]
where the time goes in v5:
time: 401 us; the launch traced here: 395 us
  Pallas kernels  238 us (59%)
  local copies, waits for them, and re-layouts  74.8 us (19%)
  other arithmetic  49.9 us (12%)
  matrix products  31.4 us (8%)
    pallas_call x5, Pallas kernels, swap(): pl.pallas_call(functools.partial(swap_kernel, plan), in_specs=[pl.BlockSp...  109 us
    pallas_call x1, Pallas kernels, front(): pl.pallas_call(functools.partial(front_kernel, dp == 2), in_specs=[anywhe...  79.2 us
    pallas_call x1, Pallas kernels, back(): pl.pallas_call(back_kernel, in_specs=[vmem] * 4 + [anywhere], out_specs=[...  49.1 us
    dot_general x11, matrix products, dot(): lax.dot_general(a, b, (((ca,), (cb,)), ((), ())), preferred_element_type=...  31.4 us
    unnamed x93, local copies, waits for them, and re-layouts  19.4 us
    another operation x2, local copies, waits for them, and re-layouts, in_halves(): return padded(array.reshape(shape), axis + 1, to).reshape(flat)  11.1 us
    pad x11, local copies, waits for them, and re-layouts, padded(): return jnp.pad(array, widths)  9.24 us
    another operation x2, other arithmetic  8.16 us

profile of v5, /device:TPU:0, one launch (start us, length us, event | category | flops | bytes accessed | tf_op | source)
XLA Modules:
  0.0 395.1 jit_solution(11355331843819035370)
XLA Ops:
  0.7 1.4 pad.48.qkv_in
  2.0 1.1 pad.49.out_in
  3.1 1.9 pad.50.gu_in
  5.0 1.2 copy.52
  6.3 2.0 convert_element_type.386
  8.3 2.5 copy.53
  10.9 2.2 copy.51
  13.2 1.4 fusion.12
  14.6 1.4 fusion.21
  16.3 79.2 %shard_map.152 = (bf16[4,2,128,1600]{3,2,1,0:T(8,128)(2,1)}, bf16[4,2,128,960]{3,2,1,0:T(8,128)(2,1)}, bf16[4,2,128,1280]{3,2,1,0:T(8,128)(2,1)}, bf16[4,256,960...) custom-call(bf16[2,128,1600]{2,1,0:T(8,128)(2,1)S(1)} %pad.48.qkv_in, ...), custom_call_target="tpu_custom_call" | custom-call | flops 1000000000 | bytes 100000000 | tf_op jit(solution)/shard_map/pallas_call | solution.py:283
  95.6 2.5 slice.204
  99.4 1.6 copy-done.25
  101.0 1.6 slice.205
  103.5 25.4 %shard_map.153 = bf16[4,256,960]{2,1,0:T(8,128)(2,1)} custom-call(bf16[256,960]{1,0:T(8,128)(2,1)} %multiply_convert_fusion.3.refs_0_), custom_call_target="tpu_custom_call" | custom-call | bytes 39321600 | tf_op jit(solution)/shard_map/pallas_call | solution.py:130
  130.0 5.3 %fusion.35 = f32[1024,1280]{1,0:T(8,128)S(1)} fusion(bf16[1024,960]{1,0:T(8,128)(2,1)} %bitcast.176, bf16[960,1280]{1,0:T(8,128)(2,1)} %bitcast.192), kind=kOutput, calls=%fused_computation.108 | convolution fusion | flops 2516582400 | bytes 9666560 | tf_op jit(solution)/shard_map/dot_general | solution.py:23
  135.4 3.6 fusion.3
  138.9 1.1 copy-done.40
  140.4 4.0 %convolution_convert_fusion.3 = bf16[1024,960]{0,1:T(8,128)(2,1)} fusion(bf16[960,1280]{1,0:T(8,128)(2,1)S(1)} %bitcast.193, bf16[1024,640]{1,0:T(8,128)(2,1)S(1)} %get-tuple-element.88, bf16[1024,640]{1,0:T(8,128)(2,1)S(1)} %get-tuple-element.87), kind=kOutput, calls=%fused_computation.28 | convolution fusion | flops 2522808320 | bytes 7045120 | tf_op jit(solution)/shard_map/dot_general | solution.py:23
  144.4 3.9 copy.58
  148.3 4.7 %reshape.505 = bf16[1024,2,480]{2,1,0:T(2,128)(2,1)} reshape(bf16[4,256,960]{2,1,0:T(8,128)(2,1)} %get-tuple-element.38) | data formatting | bytes 3932160 | tf_op jit(solution)/shard_map/reshape;reshape | solution.py:581
  153.0 6.4 %copy.74 = bf16[1024,2,480]{0,2,1:T(8,128)(2,1)} copy(bf16[1024,2,480]{2,1,0:T(2,128)(2,1)} %reshape.505) | data formatting | bytes 3932160 | tf_op jit(solution)/shard_map/reshape;reshape | solution.py:581
  159.4 1.8 pad.52
  161.3 2.6 convolution_convert_fusion.5
  164.0 4.3 %copy.60 = bf16[4,256,960]{1,0,2:T(4,128)(2,1)} copy(bf16[4,256,960]{2,1,0:T(8,128)(2,1)} %bitcast_dynamic-update-slice_fusion) | data formatting | bytes 3932160 | tf_op jit(solution)/shard_map/jit(dynamic_update_index_in_dim)/dynamic_update_slice | solution.py:573
  168.2 4.5 %reshape_reshape.7 = bf16[1024,16,60]{0,2,1:T(8,128)(2,1)} reshape(bf16[4,256,960]{1,0,2:T(4,128)(2,1)} %copy.60) | data formatting | bytes 3932160 | tf_op jit(solution)/shard_map/reshape;reshape | solution.py:459
  172.7 2.1 pad.53
  175.1 4.2 %convolution_convert_fusion.1.refs_2_ = bf16[1024,1280]{1,0:T(8,128)(2,1)} fusion(bf16[1024,1024]{0,1:T(8,128)(2,1)S(1)} %bitcast.195, bf16[1024,640]{1,0:T(8,128)(2,1)S(1)} %copy-done.43, bf16[1024,640]{1,0:T(8,128)(2,1)S(1)} %copy-done.41), kind=kOutput, calls=%fused_computation.2 | convolution fusion | flops 2690908160 | bytes 7340032 | tf_op jit(solution)/shard_map/dot_general | solution.py:23
  179.2 26.5 %shard_map.154 = (bf16[4,256,960]{2,1,0:T(8,128)(2,1)}, bf16[4,160,1024]{2,1,0:T(8,128)(2,1)}, bf16[2,1024,640]{2,1,0:T(8,128)(2,1)}) custom-call(bf16[4,256,960]{2,1,0:T(8,128)(2,1)} %bitcast.172, bf16[4,160,1024]{2,1,0:T(8,128)(2,1)} %bitcast.200, bf16[1024,1280]{1,0:T(8,128)(2,1)} %convolution_convert_fusion.1.refs_2_), custom_call_target="tpu_custom_call" | custom-call | bytes 117964800 | tf_op jit(solution)/shard_map/pallas_call | solution.py:130
  205.8 2.4 fusion.11
  208.6 1.6 copy-done.19
  210.1 1.5 convolution_convert_fusion.6.g_ref
  211.6 3.0 convolution_convert_fusion.4
  214.7 3.9 copy.55
  218.5 1.3 copy-done.6
  219.9 1.0 copy-done.8
  220.9 1.0 copy-done.9
  221.9 49.1 %shard_map.155 = (f32[960,256]{1,0:T(8,128)S(1)}, bf16[4,2,320,256]{3,2,1,0:T(8,128)(2,1)S(1)}, bf16[4,2,320,256]{3,2,1,0:T(8,128)(2,1)S(1)}, bf16[4,256,960]{2,1,0:T(8,128)(2,1)}) custom-call(bf16[960,256]{1,0:T(8,128)(2,1)S(1)} %copy-done.8, bf16[4,2,320,256]{3,2,1,0:T(8,128)(2,1)S(1)} %copy-done.6, bf16[960,256]{1,0:T(8,128)(2,1)S(1)} %copy-done.9, ...), custom_call_target="tpu_custom_call" | custom-call | flops 10066329600 | bytes 5242880 | tf_op jit(solution)/shard_map/pallas_call | solution.py:385
  271.0 1.1 copy-done.4
  272.1 3.2 fusion.10
  275.3 2.5 copy.68
  277.8 3.8 slice.227
  281.6 1.3 add_add_fusion.3
  283.2 1.6 copy-done.22
  285.1 1.3 fusion.15
  287.2 1.3 copy.69
  289.5 3.0 convolution_convert_fusion.refs_0_
  293.8 2.1 convolution_convert_fusion.2.refs_1_
  296.7 2.4 add_convert_fusion.1
  299.1 6.0 %shard_map.156 = (bf16[2,1024,896]{2,1,0:T(8,128)(2,1)}, bf16[2,1024,512]{2,1,0:T(8,128)(2,1)}, f32[2,4,4,8,128]{4,3,2,1,0:T(8,128)}, bf16[2,160,512]{2,1,0:T(8,128)(2,1)}) custom-call(bf16[1024,1792]{1,0:T(8,128)(2,1)} %convolution_convert_fusion.refs_0_, bf16[1024,1024]{1,0:T(8,128)(2,1)} %convolution_convert_fusion.2.refs_1_, ...), custom_call_target="tpu_custom_call" | custom-call | bytes 124518400 | tf_op jit(solution)/shard_map/pallas_call | solution.py:130
  305.2 4.3 %select_bitcast_fusion.3 = (f32[1024,512]{1,0:T(8,128)}, f32[1024,512]{1,0:T(8,128)}) fusion(bf16[2,1024,512]{2,1,0:T(8,128)(2,1)} %get-tuple-element.49, pred[]{:T(512)S(6)} %eq.28, pred[]{:T(512)S(6)} %eq.29), kind=kLoop, calls=%fused_computation.26 | loop fusion | flops 2097152 | bytes 6291458 | tf_op jit(solution)/shard_map/jit(_where)/select_n | solution.py:568
  309.5 3.2 fusion.6
  312.8 3.4 select_bitcast_fusion.1
  316.2 4.9 %fusion = bf16[1024,800]{1,0:T(8,128)(2,1)S(1)} fusion(f32[1024,896]{1,0:T(8,128)} %get-tuple-element.91, f32[1024,896]{1,0:T(8,128)} %get-tuple-element.90, bf16[1024,1792]{1,0:T(8,128)(2,1)} %convolution_convert_fusion.refs_0_, s32[]{:T(128)S(6)} %select_n.482), kind=kLoop, calls=%fused_computation.4 | loop fusion | flops 3276800 | bytes 9830404 | tf_op jit(solution)/shard_map/convert.11
  321.2 2.2 pad_maximum_fusion.refs_0_
  324.0 2.7 fusion.4
  326.8 1.2 copy.78
  328.0 33.4 %shard_map.157 = (bf16[4,256,1280]{2,1,0:T(8,128)(2,1)}, f32[4,4,8,128]{3,2,1,0:T(8,128)}, bf16[4,4,64,640]{3,2,1,0:T(8,128)(2,1)}) custom-call(bf16[4,256,1280]{2,1,0:T(8,128)(2,1)} %pad_maximum_fusion.refs_0_, f32[4,4,8,128]{3,2,1,0:T(8,128)} %bitcast_add_fusion.3.refs_1_, bf16[4,4,64,640]{3,2,1,0:T(8,128)(2,1)} %bitcast.179), custom_call_target="tpu_custom_call" | custom-call | bytes 79953920 | tf_op jit(solution)/shard_map/pallas_call | solution.py:130
  361.4 1.4 select_add_fusion
  362.8 3.3 add_convert_fusion
  366.1 2.0 fusion.20.refs_2_
  368.1 17.9 %shard_map.158 = (bf16[4,64,1280]{2,1,0:T(8,128)(2,1)}, f32[4,8,128]{2,1,0:T(8,128)}, bf16[4,64,640]{2,1,0:T(8,128)(2,1)}) custom-call(bf16[4,64,1280]{2,1,0:T(8,128)(2,1)} %bitcast.184, f32[4,8,128]{2,1,0:T(8,128)} %bitcast.212, bf16[4,64,640]{2,1,0:T(8,128)(2,1)} %fusion.20.refs_2_), custom_call_target="tpu_custom_call" | custom-call | bytes 19988480 | tf_op jit(solution)/shard_map/pallas_call | solution.py:130
  387.2 1.4 add_bitcast_fusion.1
  390.0 1.5 dynamic-slice_dynamic-update-slice_fusion
  391.6 1.1 convert_bitcast_fusion
  (123 shorter events, 14.8 us)
Async XLA Ops:
  0.6 134.7 %copy-start = (bf16[640,960]{0,1:T(8,128)(2,1)S(1)}, bf16[640,960]{0,1:T(8,128)(2,1)}, u32[]{:S(2)}) copy-start(bf16[640,960]{0,1:T(8,128)(2,1)} %param.16) | copy-start | bytes 3686404
  0.7 2.5 copy-start.23
  5.0 5.8 %copy-start.36 = (f32[960]{0:T(1024)S(1)}, f32[960]{0:T(1024)}, u32[]{:S(2)}) copy-start(f32[960]{0:T(1024)} %param.11) | copy-start | bytes 11524
  13.2 3.0 copy-start.37
  95.6 3.5 copy-start.2
  95.6 3.5 copy-start.5
  95.6 3.5 copy-start.7
  95.6 2.6 copy-start.13
  98.1 1.3 copy-start.18
  98.2 2.8 copy-start.25
  99.4 108.8 %copy-start.10 = (f32[256,960]{1,0:T(8,128)}, f32[256,960]{1,0:T(8,128)S(1)}, u32[]{:S(2)}) copy-start(f32[256,960]{1,0:T(8,128)S(1)} %get-tuple-element.106) | copy-start | bytes 2949124
  101.0 1.6 copy-start.35
  130.0 5.4 %copy-start.26 = (bf16[4,256,960]{2,1,0:T(8,128)(2,1)S(1)}, bf16[4,256,960]{2,1,0:T(8,128)(2,1)}, u32[]{:S(2)}) copy-start(bf16[4,256,960]{2,1,0:T(8,128)(2,1)} %get-tuple-element.38) | copy-start | bytes 5898244
  135.4 5.1 %copy-start.24 = (bf16[4,2,120,1280]{3,2,1,0:T(8,128)(2,1)S(1)}, bf16[4,2,120,1280]{3,2,1,0:T(8,128)(2,1)}, u32[]{:S(2)}) copy-start(bf16[4,2,120,1280]{3,2,1,0:T(8,128)(2,1)} %slice.205) | copy-start | bytes 7372804
  138.9 1.1 copy-start.40
  138.9 1.5 copy-start.42
  159.4 1.9 copy-start.38
  172.7 2.2 copy-start.41
  172.7 2.3 copy-start.43
  208.2 3.4 copy-start.16
  208.2 1.9 copy-start.19
  210.1 1.5 copy-start.27
  210.1 1.5 copy-start.39
  218.5 1.3 copy-start.6
  219.9 1.0 copy-start.8
  220.9 1.0 copy-start.9
  221.9 50.2 %copy-start.11 = (f32[256,960]{1,0:T(8,128)S(1)}, f32[256,960]{1,0:T(8,128)}, u32[]{:S(2)}) copy-start(f32[256,960]{1,0:T(8,128)} %copy-done.10) | copy-start | bytes 2949124
  271.0 1.1 copy-start.4
  282.9 2.0 copy-start.22
  282.9 2.2 copy-start.14
  283.0 3.4 copy-start.31
  285.1 1.4 copy-start.12
  285.1 1.5 copy-start.17
  287.2 1.3 copy-start.20
  288.5 0.9 copy-start.32
  289.5 3.0 copy-start.3
  292.5 1.0 copy-start.28
  305.2 4.3 %copy-start.15 = (bf16[1024,1024]{1,0:T(8,128)(2,1)S(1)}, bf16[1024,1024]{1,0:T(8,128)(2,1)}, u32[]{:S(2)}) copy-start(bf16[1024,1024]{1,0:T(8,128)(2,1)} %convolution_convert_fusion.2.refs_1_) | copy-start | bytes 6291460
  309.5 3.3 copy-start.21
  321.2 2.2 copy-start.34
  362.8 3.3 copy-start.30
  391.6 3.4 copy-start.1
  392.7 1.4 copy-start.29
  392.7 1.4 copy-start.33
